TPU v7x, 512 devices: a whole 4x8x8 slice. The times are simulated.
512 devices in a mesh: snap: 8 (over z), tile: 64 (over x, y, core).
Axes of the slice: x: 4, y: 8, z: 8, core: 2. Of those that a mesh axis runs over, the one named last changes fastest.
Arguments:
- modes: bfloat16 [8192, 256], P(('snap', 'tile')), may hold values from -8 to 8
- targets: bfloat16 [8192, 256], P(('snap', 'tile')), may hold values from -16 to 16
- pairs: int32 [4096, 2], replicated, may hold values from 0 to 256, as said below
- support: int32 [4096, 256], P(('snap', 'tile')), may hold values from 0 to 1, as said below
Outputs:
- coeffs: float32 [4096, 256], P(('snap', 'tile'))
- resid: float32 [4096, 256], P(('snap', 'tile'))
Inputs may be any that keep to these rules, and one draw needn't show every extreme that they name: Rows are distinct unordered pairs; the first entry is below 256; every index below 256 is the first entry of exactly 16 rows. `support`: every target has at least one active term.
All inputs are finite; a program needn't handle non-finite values.
Results may differ from a plain program's by a relative error of at most 0.0036.
Values may be sent and summed in bfloat16 or wider, within the bound.
A program may use at most 64 MiB of HBM per device.

v0:
```python
import jax
import jax.numpy as jnp
from jax import lax
from jax.sharding import PartitionSpec as P

ITERS = 2


def widened(rows_in):
    return jnp.concatenate(
        [rows_in.astype(jnp.float32), jnp.ones((rows_in.shape[0], 1), jnp.float32)], axis=1
    )


def body(modes, targets, pairs, support):
    snap_count = lax.axis_size("snap")
    tile_count = lax.axis_size("tile")
    term_count = pairs.shape[0]
    mode_count = modes.shape[1]
    target_count = targets.shape[1]
    share_rows = term_count // (snap_count * tile_count)
    total_snaps = modes.shape[0] * snap_count * tile_count
    tile_at = lax.axis_index("tile")
    term_grid = jnp.arange(term_count, dtype=jnp.int32).reshape(snap_count, tile_count, share_rows)
    own_terms = lax.dynamic_index_in_dim(term_grid, tile_at, 1, keepdims=False).reshape(-1)
    first_factor = pairs[:, 0]
    second_factor = pairs[:, 1]
    start_sums = (
        jnp.zeros((snap_count * share_rows, term_count), jnp.float32),
        jnp.zeros((snap_count * share_rows, target_count), jnp.float32),
    )
    rows_in = lax.all_gather(modes, "tile", axis=0, tiled=True)
    count_rows = rows_in.shape[0]
    block_rows = max((divisor for divisor in range(1, 513) if count_rows % divisor == 0))

    def inner(totals, block_item):
        block_modes, block_targets = block_item
        extended = widened(block_modes)
        library = (
            jnp.take(extended, first_factor, axis=1) * jnp.take(extended, second_factor, axis=1)
        ).astype(jnp.bfloat16)
        mine = jnp.take(library, own_terms, axis=1)
        gram_sum = totals[0] + lax.dot_general(
            mine, library, (((0,), (0,)), ((), ())), preferred_element_type=jnp.float32
        )
        cross_sum = totals[1] + lax.dot_general(
            mine, block_targets, (((0,), (0,)), ((), ())), preferred_element_type=jnp.float32
        )
        return ((gram_sum, cross_sum), None)

    blocks = (
        rows_in.reshape(count_rows // block_rows, block_rows, mode_count),
        lax.all_gather(targets, "tile", axis=0, tiled=True).reshape(
            count_rows // block_rows, block_rows, target_count
        ),
    )
    results, _ = lax.scan(inner, start_sums, blocks)
    gram_part, cross_part = results
    gram_all, cross_all = lax.psum((gram_part, cross_part), "snap")
    snap_at = lax.axis_index("snap")
    gram_rows = lax.dynamic_slice_in_dim(gram_all, snap_at * share_rows, share_rows, 0)
    cross_rows = lax.dynamic_slice_in_dim(cross_all, snap_at * share_rows, share_rows, 0)
    gram_rows = gram_rows / total_snaps
    cross_rows = cross_rows / total_snaps
    support_mask = support.astype(jnp.float32)

    def energy_of(vector):
        return lax.psum(jnp.sum(vector * vector, axis=0), ("snap", "tile"))

    resid = support_mask * cross_rows
    coeffs = jnp.zeros_like(resid)
    direction = resid
    energy = energy_of(resid)
    for step in range(ITERS):
        product = jnp.dot(
            gram_rows,
            lax.all_gather(direction, ("snap", "tile"), axis=0, tiled=True),
            precision=lax.Precision.HIGHEST,
            preferred_element_type=jnp.float32,
        )
        image = support_mask * product
        step_len = energy / lax.psum(jnp.sum(direction * image, axis=0), ("snap", "tile"))
        coeffs = coeffs + step_len * direction
        resid = resid - step_len * image
        if step + 1 < ITERS:
            fresh = energy_of(resid)
            direction = resid + fresh / energy * direction
            energy = fresh
    return (coeffs, resid)


def solution(mesh):
    return jax.shard_map(
        body,
        mesh=mesh,
        in_specs=(
            P(("snap", "tile"), None),
            P(("snap", "tile"), None),
            P(),
            P(("snap", "tile"), None),
        ),
        out_specs=(P(("snap", "tile"), None), P(("snap", "tile"), None)),
        check_vma=False,
    )
```

profile of v0, /device:TPU:1, one launch (start us, length us, event | category | flops | bytes accessed | tf_op | source)
XLA Modules:
  0.0 834.8 jit_solution(8397565621540414149)
XLA Ops:
  7.3 0.9 fusion.16
  8.2 54.4 %all_gather.12 = bf16[1024,256]{1,0:T(8,128)(2,1)S(1)} all-gather(bf16[16,256]{1,0:T(8,128)(2,1)} %param.8), channel_id=1, replica_groups=mesh['snap'=8,'tile'=64] {'tile'}, dimensions={0}, use_global_device_ids=true | all-gather | bytes 532480 | tf_op jit(solution)/shard_map/all_gather | solution.py:32
  62.6 49.5 %all_gather.13 = bf16[1024,256]{1,0:T(8,128)(2,1)S(1)} all-gather(bf16[16,256]{1,0:T(8,128)(2,1)} %param.9), channel_id=1, replica_groups=mesh['snap'=8,'tile'=64] {'tile'}, dimensions={0}, use_global_device_ids=true | all-gather | bytes 532480 | tf_op jit(solution)/shard_map/all_gather | solution.py:53
  112.0 101.3 %while.13 = (s32[]{:T(128)}, f32[64,4096]{1,0:T(8,128)S(1)}, f32[64,256]{1,0:T(8,128)S(1)}, s32[64]{0:T(128)S(1)}, bf16[2,512,256]{2,1,0:T(8,128)(2,1)S(1)}, /*i...) while((s32[]{:T(128)}, f32[64,4096]{1,0:T(8,128)S(1)}, ...), condition=%wide.region_1.3_spmd.clone, body=%wide.region_0.2_spmd.clone.sunk | while | flops 294438976 | bytes 63463412 | solution.py:57
  112.3 16.9 %gather_fusion.1 = f32[4096,512]{1,0:T(8,128)} fusion(f32[512,257]{0,1:T(8,128)S(1)} %pad_convert_fusion.2, s32[4096]{0:T(1024)S(1)} %get-tuple-element.170), kind=kCustom, calls=%fused_computation.clone.clone.1 | custom fusion | bytes 16793600 | tf_op jit(solution)/shard_map/while/body/eval_jaxpr/jit(_take)/gather | solution.py:40
  129.2 16.9 %gather_fusion = f32[4096,512]{1,0:T(8,128)} fusion(f32[512,257]{0,1:T(8,128)S(1)} %pad_convert_fusion.2, s32[4096]{0:T(1024)S(1)} %get-tuple-element.169), kind=kCustom, calls=%fused_computation.1.clone.clone.1 | custom fusion | bytes 16793600 | tf_op jit(solution)/shard_map/while/body/eval_jaxpr/jit(_take)/gather | solution.py:40
  146.1 9.2 %fusion.28 = bf16[512,4096]{0,1:T(8,128)(2,1)} fusion(f32[4096,512]{1,0:T(8,128)} %gather_fusion, f32[4096,512]{1,0:T(8,128)} %gather_fusion.1, pred[4096]{0:T(1024)(128)(4,1)S(1)} %get-tuple-element.171, pred[4096]{0:T(1024)(128)(4,1)S(1)} %get-tuple-element.172), kind=kLoop, calls=%fused_computation.4.clone.1 | loop fusion | flops 8388608 | bytes 20979712 | tf_op jit(solution)/shard_map/while/body/eval_jaxpr/convert_element_type | solution.py:41
  155.3 3.4 gather_fusion.2
  158.8 3.7 convolution_add_fusion.4
  163.0 16.9 %gather_fusion.1 = f32[4096,512]{1,0:T(8,128)} fusion(f32[512,257]{0,1:T(8,128)S(1)} %pad_convert_fusion.2, s32[4096]{0:T(1024)S(1)} %get-tuple-element.170), kind=kCustom, calls=%fused_computation.clone.clone.1 | custom fusion | bytes 16793600 | tf_op jit(solution)/shard_map/while/body/eval_jaxpr/jit(_take)/gather | solution.py:40
  179.8 16.9 %gather_fusion = f32[4096,512]{1,0:T(8,128)} fusion(f32[512,257]{0,1:T(8,128)S(1)} %pad_convert_fusion.2, s32[4096]{0:T(1024)S(1)} %get-tuple-element.169), kind=kCustom, calls=%fused_computation.1.clone.clone.1 | custom fusion | bytes 16793600 | tf_op jit(solution)/shard_map/while/body/eval_jaxpr/jit(_take)/gather | solution.py:40
  196.7 9.2 %fusion.28 = bf16[512,4096]{0,1:T(8,128)(2,1)} fusion(f32[4096,512]{1,0:T(8,128)} %gather_fusion, f32[4096,512]{1,0:T(8,128)} %gather_fusion.1, pred[4096]{0:T(1024)(128)(4,1)S(1)} %get-tuple-element.171, pred[4096]{0:T(1024)(128)(4,1)S(1)} %get-tuple-element.172), kind=kLoop, calls=%fused_computation.4.clone.1 | loop fusion | flops 8388608 | bytes 20979712 | tf_op jit(solution)/shard_map/while/body/eval_jaxpr/convert_element_type | solution.py:41
  205.9 3.4 gather_fusion.2
  209.4 3.7 convolution_add_fusion.4
  213.4 1.0 copy-done
  214.4 77.7 %all-reduce.5.cloned.1.call-done = (f32[64,256]{1,0:T(8,128)}, f32[64,4096]{1,0:T(8,128)}) async-done(((f32[64,256]{1,0:T(8,128)}, f32[64,4096]{1,0:T(8,128)}), (f32[64,256]{1,0:T(8,128)}, f32[64,4096]{1,0:T(8,128)})) %all-reduce.5.cloned.1.call-update) | async-done | bytes 1114128 | tf_op jit(solution)/shard_map/psum | solution.py:59
  292.2 1.3 multiply_multiply_fusion
  293.5 124.9 %all-gather.3.cloned.1.call-done = f32[4096,256]{1,0:T(8,128)} async-done(((f32[8,256]{1,0:T(8,128)}), f32[4096,256]{1,0:T(8,128)}) %all-gather.3.cloned.1.call-update) | async-done | bytes 4194320 | tf_op jit(solution)/shard_map/all_gather | solution.py:77
  418.5 3.9 multiply_reduce_fusion.2
  422.4 96.1 %all-reduce.1 = (f32[256]{0:T(256)S(1)}, f32[256]{0:T(256)S(1)}) all-reduce(f32[256]{0:T(256)S(1)} %get-tuple-element.84, f32[256]{0:T(256)S(1)} %get-tuple-element.83), channel_id=1, replica_groups=mesh['snap'=8,'tile'=64] {'snap','tile'}, use_global_device_ids=true, to_apply=%region_4.6 | all-reduce | flops 512 | bytes 4096 | tf_op jit(solution)/shard_map/psum | solution.py:68
  518.6 93.8 %psum.46 = f32[256]{0:T(256)S(1)} all-reduce(f32[256]{0:T(256)S(1)} %multiply_reduce_fusion.1), channel_id=1, replica_groups=mesh['snap'=8,'tile'=64] {'snap','tile'}, use_global_device_ids=true, to_apply=%region_9.11 | all-reduce | flops 256 | bytes 2048 | tf_op jit(solution)/shard_map/psum | solution.py:68
  613.0 114.6 %all-gather.5.cloned.1.call-done = f32[4096,256]{1,0:T(8,128)} async-done(((f32[8,256]{1,0:T(8,128)}), f32[4096,256]{1,0:T(8,128)}) %all-gather.5.cloned.1.call-update) | async-done | bytes 4194320 | tf_op jit(solution)/shard_map/all_gather | solution.py:77
  727.6 3.9 multiply_reduce_fusion
  731.5 96.2 %psum.47 = f32[256]{0:T(256)S(1)} all-reduce(f32[256]{0:T(256)S(1)} %get-tuple-element.114), channel_id=1, replica_groups=mesh['snap'=8,'tile'=64] {'snap','tile'}, use_global_device_ids=true, to_apply=%region_11.13 | all-reduce | flops 256 | bytes 2048 | tf_op jit(solution)/shard_map/psum | solution.py:82
  (43 shorter events, 2.5 us)
Async XLA Ops:
  7.2 285.0 %all-reduce.5.cloned.1.call-start = ((), (), s32[]{:S(2)}) async-start(), calls=%async_computation.2 | async-start | bytes 2228224 | tf_op jit(solution)/shard_map/psum | solution.py:59
  112.0 180.1 %copy-start.4 = (s32[8,256]{1,0:T(8,128)S(1)}, s32[8,256]{1,0:T(8,128)}, u32[]{:S(2)}) copy-start(s32[8,256]{1,0:T(8,128)} %param.11) | copy-start | bytes 24580
  213.3 1.0 copy-start
  213.3 1.0 copy-start.1
  214.4 204.1 %all-gather.3.cloned.1.call-start = ((), (), s32[]{:S(2)}) async-start(), calls=%async_computation | async-start | bytes 4202496 | tf_op jit(solution)/shard_map/all_gather | solution.py:77
  293.5 225.1 %copy-start.2 = (f32[8,256]{1,0:T(8,128)S(1)}, f32[8,256]{1,0:T(8,128)}, u32[]{:S(2)}) copy-start(f32[8,256]{1,0:T(8,128)} %multiply_multiply_fusion) | copy-start | bytes 24580
  293.5 434.1 %all-gather.5.cloned.1.call-start = ((), (), s32[]{:S(2)}) async-start(), calls=%async_computation.1 | async-start | bytes 4202496 | tf_op jit(solution)/shard_map/all_gather | solution.py:77
  613.0 214.7 %copy-start.3 = (f32[8,256]{1,0:T(8,128)S(1)}, f32[8,256]{1,0:T(8,128)}, u32[]{:S(2)}) copy-start(f32[8,256]{1,0:T(8,128)} %multiply_add_fusion.1) | copy-start | bytes 24580
Sparse Core Ops, SparseCore 0:
  214.5 77.6 all-reduce.4
  297.6 120.7 all-gather.2
  613.1 114.4 all-gather.4
where the time goes:
time: 835 us
  blocking collectives  390 us (47%)
  waiting for transfers between devices  317 us (38%)
  local copies, waits for them, and re-layouts  76.7 us (9%)
  other arithmetic  21.2 us (3%)
  matrix products  15.7 us (2%)
  between operations  13.8 us (2%)
    all_gather x2, waiting for transfers between devices, body(): lax.all_gather(direction, ('snap', 'tile'), axis=0, tiled=True)  239 us
    psum x2, blocking collectives, energy_of(): return lax.psum(jnp.sum(vector * vector, axis=0), ('snap', 'tile'))  190 us
    psum x1, blocking collectives, body(): lax.psum(jnp.sum(direction * image, axis=0), ('snap', 'tile'))  96.2 us
    psum x1, waiting for transfers between devices, body(): gram_all, cross_all = lax.psum((gram_part, cross_part), 'snap')  77.7 us
    all_gather x1, blocking collectives, body(): rows_in = lax.all_gather(modes, 'tile', axis=0, tiled=True)  54.4 us
    all_gather x1, blocking collectives, body(): lax.all_gather(targets, 'tile', axis=0, tiled=True)  49.5 us
    gather x2, local copies, waits for them, and re-layouts, inner(): jnp.take(extended, first_factor, axis=1)  33.8 us
    gather x2, local copies, waits for them, and re-layouts, inner(): jnp.take(extended, second_factor, axis=1)  33.7 us
  transfers between devices with their start and end apart: 3, of which 3 were waited for; matrix products, arithmetic and copies ran while one was open for 0% of the time, Pallas kernels for 0%

commit v1 on v0

v1 whole, which is shorter than its diff:
```python
import jax
import jax.numpy as jnp
from jax import lax
from jax.experimental import pallas as pl
from jax.experimental.pallas import tpu as pltpu
from jax.sharding import PartitionSpec as P

NX, NY, NZ, NC = 4, 8, 8, 2
RING = NZ * NC
PLANE = NX * NY
MODES = 256
TARGETS = 256
TERMS = 4096
ROWS = 16
SNAPS = 8192
LOCAL = PLANE * ROWS
OWN = TERMS // RING
GROUP = TARGETS // PLANE
CHUNK = 1024
F32 = jnp.float32
BF16 = jnp.bfloat16
MESH = pl.DeviceIdType.MESH


def split(value):
    high = value.astype(BF16)
    low = (value - high.astype(F32)).astype(BF16)
    return jnp.concatenate([high, low], axis=0)


def merge(value):
    return value[:GROUP] + value[GROUP:]


def dot_nt(lhs, rhs):
    return lax.dot_general(lhs, rhs, (((1,), (1,)), ((), ())), preferred_element_type=F32)


def dot_nn(lhs, rhs):
    return jnp.dot(lhs, rhs, preferred_element_type=F32)


def iota(shape, dim):
    return lax.broadcasted_iota(jnp.int32, shape, dim)


def drain(ref, sem):
    pltpu.make_async_copy(ref, ref, sem).wait()


def kernel(
    modes_ref, targets_ref, pairs_ref, support_ref, coeffs_ref, resid_ref,
    rows, extra, hot_a, hot_b, terms, library,
    part0, part1, part2, got0, got1, got2, full0, full1,
    curve1, curve2, curves1, curves2, turn_x, got_x, turn_y, got_y,
    send_sem, recv_sem,
):
    z = lax.axis_index("snap")
    tile = lax.axis_index("tile")
    x = tile // (NY * NC)
    y = (tile // NC) % NY
    core = tile % NC
    spot = x * NY + y
    me = z * NC + core

    def at_x(step):
        other = lax.rem(x + step, NX)
        return other, (z, (other * NY + y) * NC + core)

    def at_y(step):
        other = lax.rem(y + step, NY)
        return other, (z, (x * NY + other) * NC + core)

    def at_ring(step):
        other = lax.rem(me + step, RING)
        return other, (other // NC, spot * NC + lax.rem(other, NC))

    barrier = pltpu.get_barrier_semaphore()
    for step in range(1, NY):
        pl.semaphore_signal(barrier, inc=1, device_id=at_y(step)[1], device_id_type=MESH)
    for step in range(1, NX):
        pl.semaphore_signal(barrier, inc=1, device_id=at_x(step)[1], device_id_type=MESH)
    for step in range(1, RING):
        pl.semaphore_signal(barrier, inc=1, device_id=at_ring(step)[1], device_id_type=MESH)

    def send(src, dst, stage, device):
        pltpu.make_async_remote_copy(
            src_ref=src, dst_ref=dst, send_sem=send_sem.at[stage], recv_sem=recv_sem.at[stage],
            device_id=device, device_id_type=MESH,
        ).start()

    own_rows = pl.ds(pl.multiple_of(spot * ROWS, ROWS), ROWS)
    slab = pl.ds(pl.multiple_of(x * (NY * ROWS), NY * ROWS), NY * ROWS)
    rows[own_rows, :] = modes_ref[...]
    extra[own_rows, 0:TARGETS] = targets_ref[...]
    active = support_ref[...].astype(F32)
    extra[own_rows, TARGETS:] = jnp.concatenate(
        [active[:, :128], active[:, 128:]], axis=0
    ).astype(BF16)
    pl.semaphore_wait(barrier, NY - 1 + NX - 1 + RING - 1)

    for step in range(1, NY):
        send(rows.at[own_rows], rows.at[own_rows], 0, at_y(step)[1])
    for step in range(1, NY):
        send(extra.at[own_rows], extra.at[own_rows], 1, at_y(step)[1])

    pairs = pairs_ref[...].astype(F32)
    stacked = jnp.concatenate(
        [pairs[side : side + 1, 512 * k : 512 * k + 512] for side in (0, 1) for k in range(NZ)],
        axis=0,
    ).astype(BF16)
    place = iota((512, 512), 1)
    origin = (place % 256) // 8 * 16 + place // 256 * 8 + place % 8
    order = (iota((512, 512), 0) == origin).astype(F32).astype(BF16)
    terms[...] = dot_nn(stacked, order).astype(jnp.int32)
    for k in range(NZ):
        span = slice(512 * k, 512 * k + 512)
        index = iota((MODES, 512), 0)
        hot_a[:, span] = (index == terms[k : k + 1, :]).astype(F32).astype(BF16)
        hot_b[:, span] = (index == terms[NZ + k : NZ + k + 1, :]).astype(F32).astype(BF16)

    drain(rows.at[pl.ds(0, (NY - 1) * ROWS)], recv_sem.at[0])
    for step in range(1, NX):
        send(rows.at[slab], rows.at[slab], 2, at_x(step)[1])
    drain(extra.at[pl.ds(0, (NY - 1) * ROWS)], recv_sem.at[1])
    for step in range(1, NX):
        send(extra.at[slab], extra.at[slab], 3, at_x(step)[1])
    drain(rows.at[pl.ds(0, (NX - 1) * NY * ROWS)], recv_sem.at[2])

    for k in range(TERMS // CHUNK):
        span = slice(k * CHUNK, (k + 1) * CHUNK)
        per = CHUNK // 512
        constant = jnp.concatenate(
            [terms[NZ + k * per + j : NZ + k * per + j + 1, :] for j in range(per)], axis=1
        )
        constant = (constant == MODES).astype(F32)
        first = dot_nn(rows[...], hot_a[:, span])
        second = dot_nn(rows[...], hot_b[:, span]) + constant
        library[:, span] = (first * second).astype(BF16)

    drain(extra.at[pl.ds(0, (NX - 1) * NY * ROWS)], recv_sem.at[3])

    group = y * NX + x
    pick = (iota((2 * GROUP, TARGETS), 1) == group * GROUP + iota((2 * GROUP, TARGETS), 0)) & (
        iota((2 * GROUP, TARGETS), 0) < GROUP
    )
    wanted = dot_nt(pick.astype(F32).astype(BF16), extra[:, 0:TARGETS]).astype(BF16)
    half = group // (PLANE // 2)
    column = group % (PLANE // 2) * GROUP
    pick = (iota((2 * GROUP, 128), 1) == column + iota((2 * GROUP, 128), 0)) & (
        iota((2 * GROUP, 128), 0) < GROUP
    )
    flags = dot_nt(pick.astype(F32).astype(BF16), extra[:, TARGETS:]).astype(BF16)
    lane = iota((512, 256), 1)
    pick = iota((512, 256), 0) == lane // 8 * 16 + half * 8 + lane % 8
    mask = dot_nn(flags, pick.astype(F32).astype(BF16))[:GROUP]

    own_terms = pl.ds(pl.multiple_of(me * OWN, OWN), OWN)

    def scatter_sums(value, part, got, stage):
        part[...] = value
        for step in range(1, RING):
            other, device = at_ring(step)
            theirs = pl.ds(pl.multiple_of(other * OWN, OWN), OWN)
            send(part.at[:, theirs], got.at[step - 1], stage, device)

    def sum_up(part, got, stage):
        drain(got, recv_sem.at[stage])
        total = part[:, own_terms]
        for step in range(1, RING):
            total = total + got[step - 1]
        return total * mask * (1.0 / SNAPS)

    def gather_terms(value, full, stage):
        full[:, own_terms] = value
        for step in range(1, RING):
            send(full.at[:, own_terms], full.at[:, own_terms], stage, at_ring(step)[1])
        drain(full.at[:, pl.ds(0, TERMS - OWN)], recv_sem.at[stage])
        return full[...]

    def apply(vector, curve, curves, part, got, stage):
        image = merge(dot_nt(split(vector), library[...]))
        curve[...] = jnp.broadcast_to(jnp.sum(image * image, axis=1, keepdims=True), (GROUP, 128))
        for step in range(1, RING):
            send(curve, curves.at[step - 1], stage, at_ring(step)[1])
        scatter_sums(merge(dot_nn(split(image), library[...])), part, got, stage + 1)
        drain(curves, recv_sem.at[stage])
        total = curve[...]
        for step in range(1, RING):
            total = total + curves[step - 1]
        return total[:, 0:1] * (1.0 / SNAPS), sum_up(part, got, stage + 1)

    def squares(vector):
        return jnp.sum(vector * vector, axis=1, keepdims=True)

    scatter_sums(dot_nn(wanted, library[...])[:GROUP], part0, got0, 4)
    direction = sum_up(part0, got0, 4)
    whole = gather_terms(direction, full0, 5)
    energy = squares(whole)
    curvature, product = apply(whole, curve1, curves1, part1, got1, 6)
    step_len = energy / curvature
    coeffs = step_len * direction
    resid = direction - step_len * product
    whole_resid = gather_terms(resid, full1, 8)
    fresh = squares(whole_resid)
    ratio = fresh / energy
    direction = resid + ratio * direction
    whole = whole_resid + ratio * whole
    curvature, product = apply(whole, curve2, curves2, part2, got2, 9)
    step_len = fresh / curvature
    coeffs = coeffs + step_len * direction
    resid = resid - step_len * product

    lane = iota((GROUP, 128), 1)
    for k in range(NX):
        pair = slice(k // 2 * 128, k // 2 * 128 + 128)
        left, right = coeffs[:, pair], resid[:, pair]
        if k % 2 == 0:
            right = pltpu.roll(right, 64, 1)
        else:
            left = pltpu.roll(left, 64, 1)
        turn_x[8 * k : 8 * k + 8, :] = jnp.where(lane < 64, left, right)
    at = pl.ds(pl.multiple_of(x * 8, 8), 8)
    for step in range(1, NX):
        other, device = at_x(step)
        send(turn_x.at[pl.ds(pl.multiple_of(other * 8, 8), 8)], got_x.at[at], 11, device)
    got_x[at, :] = turn_x[at, :]
    drain(got_x.at[pl.ds(0, (NX - 1) * 8)], recv_sem.at[11])
    held = got_x[...]
    square = jnp.concatenate(
        [held, pltpu.roll(held, 64, 1), jnp.zeros((64, 128), F32)], axis=0
    )
    turn_y[...] = square.T[:64]
    at = pl.ds(pl.multiple_of(y * 8, 8), 8)
    for step in range(1, NY):
        other, device = at_y(step)
        send(turn_y.at[pl.ds(pl.multiple_of(other * 8, 8), 8)], got_y.at[at], 12, device)
    got_y[at, :] = turn_y[at, :]
    drain(got_y.at[pl.ds(0, (NY - 1) * 8)], recv_sem.at[12])
    for half_at in range(2):
        left = jnp.zeros((8, 128), F32)
        right = left
        for k in range(4):
            block = got_y[8 * (4 * half_at + k) : 8 * (4 * half_at + k) + 8, :]
            here = lane // 32 == k
            left = jnp.where(here, pltpu.roll(block, 32 * k, 1) if k else block, left)
            shift = (32 * k - 32) % 128
            right = jnp.where(here, pltpu.roll(block, shift, 1) if shift else block, right)
        coeffs_ref[:, 128 * half_at : 128 * half_at + 128] = left
        resid_ref[:, 128 * half_at : 128 * half_at + 128] = right

    drain(rows.at[pl.ds(0, (NY - 1) * ROWS)], send_sem.at[0])
    drain(extra.at[pl.ds(0, (NY - 1) * ROWS)], send_sem.at[1])
    drain(rows.at[pl.ds(0, (NX - 1) * NY * ROWS)], send_sem.at[2])
    drain(extra.at[pl.ds(0, (NX - 1) * NY * ROWS)], send_sem.at[3])
    for stage, got in ((4, got0), (7, got1), (10, got2), (6, curves1), (9, curves2)):
        drain(got, send_sem.at[stage])
    for stage, full in ((5, full0), (8, full1)):
        drain(full.at[:, pl.ds(0, TERMS - OWN)], send_sem.at[stage])
    drain(got_x.at[pl.ds(0, (NX - 1) * 8)], send_sem.at[11])
    drain(got_y.at[pl.ds(0, (NY - 1) * 8)], send_sem.at[12])


def body(modes, targets, pairs, support):
    vmem = pl.BlockSpec(memory_space=pltpu.VMEM)
    out = jax.ShapeDtypeStruct(support.shape, F32)
    return pl.pallas_call(
        kernel,
        out_shape=(out, out),
        in_specs=[vmem] * 4,
        out_specs=(vmem, vmem),
        scratch_shapes=[
            pltpu.VMEM((LOCAL, MODES), BF16),
            pltpu.VMEM((LOCAL, TARGETS + 128), BF16),
            pltpu.VMEM((MODES, TERMS), BF16),
            pltpu.VMEM((MODES, TERMS), BF16),
            pltpu.VMEM((2 * NZ, 512), jnp.int32),
            pltpu.VMEM((LOCAL, TERMS), BF16),
        ]
        + [pltpu.VMEM((GROUP, TERMS), F32)] * 3
        + [pltpu.VMEM((RING - 1, GROUP, OWN), F32)] * 3
        + [pltpu.VMEM((GROUP, TERMS), F32)] * 2
        + [pltpu.VMEM((GROUP, 128), F32)] * 2
        + [pltpu.VMEM((RING - 1, GROUP, 128), F32)] * 2
        + [pltpu.VMEM((NX * 8, 128), F32)] * 2
        + [pltpu.VMEM((NY * 8, 128), F32)] * 2
        + [pltpu.SemaphoreType.DMA((13,))] * 2,
        compiler_params=pltpu.CompilerParams(
            collective_id=0, has_side_effects=True, vmem_limit_bytes=48 * 2**20
        ),
        name="regression",
    )(modes, targets, pairs.T, support)


def solution(mesh):
    rows = P(("snap", "tile"), None)
    return jax.shard_map(
        body,
        mesh=mesh,
        in_specs=(rows, rows, P(), rows),
        out_specs=(rows, rows),
        check_vma=False,
    )
```

time: 835 us -> 78.6 us (0.09)
  blocking collectives: 390 us -> 0 us
  waiting for transfers between devices: 317 us -> 0 us
  Pallas kernels: 0 us -> 73.6 us
  local copies, waits for them, and re-layouts: 76.7 us -> 4.04 us
  other arithmetic: 21.2 us -> 0 us
  matrix products: 15.7 us -> 0 us
  between operations: 13.8 us -> 0.65 us
    psum x3 -> x0, blocking collectives: 286 us -> none  [the longest x2 190 us: energy_of(): return lax.psum(jnp.sum(vector * vector, axis=0), ('snap', 'tile'))]
    all_gather x2 -> x0, waiting for transfers between devices: 239 us -> none  [body(): lax.all_gather(direction, ('snap', 'tile'), axis=0, tiled=True)]
    all_gather x2 -> x0, blocking collectives: 104 us -> none  [the longest x1 54.4 us: body(): rows_in = lax.all_gather(modes, 'tile', axis=0, tiled=True)]
    psum x1 -> x0, waiting for transfers between devices: 77.7 us -> none  [body(): gram_all, cross_all = lax.psum((gram_part, cross_part), 'snap')]
    gather x6 -> x0, local copies, waits for them, and re-layouts: 74.4 us -> none  [the longest x2 33.8 us: inner(): jnp.take(extended, first_factor, axis=1)]
    pallas_call x0 -> x1, Pallas kernels: none -> 73.6 us  [body(): pl.pallas_call(kernel, out_shape=(out, out), in_specs=[vmem] * 4, out_spe...]
    convert_element_type x2 -> x0, other arithmetic: 18.4 us -> none  [inner(): library = (jnp.take(extended, first_factor, axis=1) * jnp.take(extended,...]
    dot_general x6 -> x0, matrix products: 15.7 us -> none  [the longest x2 7.87 us: body(): jnp.dot(gram_rows, lax.all_gather(direction, ('snap', 'tile'), axis=0, ti...]
  transfers between devices with their start and end apart: 3 -> 0, of which waited for: 3 -> 0; matrix products, arithmetic and copies ran while one was open for 0% -> 0% of each run, Pallas kernels for 0% -> 0%
where the time goes in v1:
time: 78.6 us; the launch traced here: 78.3 us
  Pallas kernels  73.6 us (94%)
  local copies, waits for them, and re-layouts  4.04 us (5%)
    pallas_call x1, Pallas kernels, body(): pl.pallas_call(kernel, out_shape=(out, out), in_specs=[vmem] * 4, out_spe...  73.6 us
    unnamed x10, local copies, waits for them, and re-layouts  4.04 us

profile of v1, /device:TPU:1, one launch (start us, length us, event | category | flops | bytes accessed | tf_op | source)
XLA Modules:
  0.0 78.3 jit_solution(3377807713470051515)
XLA Ops:
  0.6 0.0 copy-start
  0.6 0.7 copy-done
  1.4 0.0 copy-start.1
  1.4 0.7 copy-done.1
  2.1 0.0 copy-start.2
  2.1 0.7 copy-done.2
  2.8 0.0 copy-start.3
  2.8 0.7 copy-done.3
  3.5 73.6 %regression.1 = (f32[8,256]{1,0:T(8,128)S(1)}, f32[8,256]{1,0:T(8,128)S(1)}) custom-call(bf16[16,256]{1,0:T(8,128)(2,1)S(1)} %copy-done.1, bf16[16,256]{1,0:T(8,128)(2,1)S(1)} %copy-done.2, s32[2,4096]{1,0:T(2,128)S(1)} %bitcast.1, s32[8,256]{1,0:T(8,128)S(1)} %copy-done.3), custom_call_target="tpu_custom_call" | custom-call | tf_op jit(solution)/shard_map/regression/pallas_call | solution.py:267
  77.1 0.6 copy.8
  77.7 0.6 copy.9
Async XLA Ops:
  0.6 0.8 copy-start
  1.4 0.7 copy-start.1
  2.1 0.7 copy-start.2
  2.8 0.7 copy-start.3

commit v2 on v0

v2 whole, which is shorter than its diff:
```python
import jax
import jax.numpy as jnp
from jax import lax
from jax.experimental import pallas as pl
from jax.experimental.pallas import tpu as pltpu
from jax.sharding import PartitionSpec as P

NX, NY, NZ, NC = 4, 8, 8, 2
RING = NZ * NC
PLANE = NX * NY
MODES = 256
TARGETS = 256
TERMS = 4096
ROWS = 16
SNAPS = 8192
SLAB = NY * ROWS
LOCAL = PLANE * ROWS
OWN = TERMS // RING
HALF = TERMS // NC
GROUP = TARGETS // PLANE
CHUNK = 1024
FAR_FIRST = (4, 3, 5, 2, 6, 1, 7)
NEAR_FIRST = (1, 7, 2, 6, 3, 5, 4)
F32 = jnp.float32
BF16 = jnp.bfloat16
MESH = pl.DeviceIdType.MESH

EXTRA, SLABS, COMPACT, PAIR, SUMS, SLICES, HALVES, CURVE, TURN = 7, 8, 11, 12, 15, 18, 20, 22, 23
STAGES = 24


def split(value):
    high = value.astype(BF16)
    low = (value - high.astype(F32)).astype(BF16)
    return jnp.concatenate([high, low], axis=0)


def merge(value):
    return value[:GROUP] + value[GROUP:]


def dot_nt(lhs, rhs):
    return lax.dot_general(lhs, rhs, (((1,), (1,)), ((), ())), preferred_element_type=F32)


def dot_nn(lhs, rhs):
    return jnp.dot(lhs, rhs, preferred_element_type=F32)


def iota(shape, dim):
    return lax.broadcasted_iota(jnp.int32, shape, dim)


def chosen(condition):
    return condition.astype(F32).astype(BF16)


def drain(ref, sem):
    pltpu.make_async_copy(ref, ref, sem).wait()


def kernel(
    modes_ref, targets_ref, pairs_ref, support_ref, out_ref,
    targets_in, pairs_in, support_in, rows, extra, compact, compact_in,
    hot_a, hot_b, terms, library,
    out0, out1, out2, pair0, pair1, pair2, pre0, pre1, pre2, got0, got1, got2,
    full0, full1, curve, curves, turn, square, turned,
    load_sem, send_sem, recv_sem,
):
    z = lax.axis_index("snap")
    tile = lax.axis_index("tile")
    x = tile // (NY * NC)
    y = (tile // NC) % NY
    core = tile % NC

    def at_plane(step_x, step_y):
        return z, (lax.rem(x + step_x, NX) * NY + lax.rem(y + step_y, NY)) * NC + core

    def at_line(step):
        other = lax.rem(z + step, NZ)
        return other, (other, tile)

    sibling = (z, tile + 1 - 2 * core)

    own_block = pl.ds(pl.multiple_of(y * ROWS, ROWS), ROWS)
    loads = [
        pltpu.make_async_copy(modes_ref, rows.at[own_block], load_sem.at[0]),
        pltpu.make_async_copy(targets_ref, targets_in, load_sem.at[1]),
        pltpu.make_async_copy(support_ref, support_in, load_sem.at[2]),
        pltpu.make_async_copy(pairs_ref, pairs_in, load_sem.at[3]),
    ]
    for load in loads:
        load.start()

    barrier = pltpu.get_barrier_semaphore()
    peers = [(a, b) for a in range(NX) for b in range(NY) if a or b]
    for a, b in peers:
        pl.semaphore_signal(barrier, inc=1, device_id=at_plane(a, b), device_id_type=MESH)
    for step in range(1, NZ):
        pl.semaphore_signal(barrier, inc=1, device_id=at_line(step)[1], device_id_type=MESH)
    pl.semaphore_signal(barrier, inc=1, device_id=sibling, device_id_type=MESH)

    def send(src, dst, stage, device, arrive=None):
        pltpu.make_async_remote_copy(
            src_ref=src, dst_ref=dst, send_sem=send_sem.at[stage],
            recv_sem=recv_sem.at[stage if arrive is None else arrive],
            device_id=device, device_id_type=MESH,
        ).start()

    for load in loads[:3]:
        load.wait()
    extra[own_block, 0:TARGETS] = targets_in[...]
    active = support_in[...].astype(F32)
    extra[own_block, TARGETS:] = jnp.concatenate(
        [active[:, :128], active[:, 128:]], axis=0
    ).astype(BF16)
    pl.semaphore_wait(barrier, len(peers) + NZ - 1 + 1)

    for step in FAR_FIRST:
        send(rows.at[own_block], rows.at[own_block], 0, at_plane(0, step), step - 1)

    def forward(block):
        source = pl.multiple_of(block * ROWS, ROWS)
        for step in (2, 1, 3):
            target = pl.multiple_of(step * SLAB + block * ROWS, ROWS)
            send(
                rows.at[pl.ds(source, ROWS)], rows.at[pl.ds(target, ROWS)], SLABS + step - 1,
                at_plane(step, 0),
            )

    forward(y)
    for step in FAR_FIRST:
        send(extra.at[own_block], extra.at[own_block], EXTRA, at_plane(0, step))

    loads[3].wait()
    pairs = pairs_in[...].astype(F32)
    stacked = jnp.concatenate(
        [pairs[side : side + 1, 512 * k : 512 * k + 512] for side in (0, 1) for k in range(NZ)],
        axis=0,
    ).astype(BF16)
    place = iota((512, 512), 1)
    origin = (place % 256) // 8 * 16 + place // 256 * 8 + place % 8
    terms[...] = dot_nn(stacked, chosen(iota((512, 512), 0) == origin)).astype(jnp.int32)
    index = iota((MODES, OWN), 0)

    def make_hot(c):
        for k in range(NZ):
            from_lane = slice(OWN * c, OWN * c + OWN)
            span = slice(HALF * c + OWN * k, HALF * c + OWN * k + OWN)
            hot_a[:, span] = chosen(index == terms[k : k + 1, from_lane])
            hot_b[:, span] = chosen(index == terms[NZ + k : NZ + k + 1, from_lane])

    make_hot(0)
    for step in NEAR_FIRST:
        drain(rows.at[pl.ds(0, ROWS)], recv_sem.at[step - 1])
        forward(lax.rem(y - step + NY, NY))
    make_hot(1)

    drain(extra.at[pl.ds(0, (NY - 1) * ROWS)], recv_sem.at[EXTRA])
    line = iota((NX * ROWS, TARGETS), 0)
    wanted = (NX * y + line // ROWS) * GROUP + line % ROWS
    pick_targets = chosen((iota((NX * ROWS, TARGETS), 1) == wanted) & (line % ROWS < GROUP))
    line = iota((NX * ROWS, 128), 0)
    wanted = (NX * (y % 4) + line // ROWS) * GROUP + line % ROWS - GROUP
    pick_flags = chosen((iota((NX * ROWS, 128), 1) == wanted) & (line % ROWS >= GROUP))
    compact[...] = (
        dot_nt(pick_targets, extra[:, 0:TARGETS]) + dot_nt(pick_flags, extra[:, TARGETS:])
    ).astype(BF16)
    for step in (2, 1, 3):
        theirs = pl.ds(pl.multiple_of(lax.rem(x + step, NX) * ROWS, ROWS), ROWS)
        send(
            compact.at[theirs], compact_in.at[pl.ds(step * ROWS, ROWS)], COMPACT,
            at_plane(step, 0),
        )
    compact_in[0:ROWS, :] = compact[pl.ds(pl.multiple_of(x * ROWS, ROWS), ROWS), :]

    def build(begin, end):
        for k in range(TERMS // CHUNK):
            span = slice(k * CHUNK, (k + 1) * CHUNK)
            c, first_z = k * CHUNK // HALF, k * CHUNK % HALF // OWN
            constant = jnp.concatenate(
                [
                    terms[NZ + j : NZ + j + 1, OWN * c : OWN * c + OWN]
                    for j in range(first_z, first_z + CHUNK // OWN)
                ],
                axis=1,
            )
            constant = (constant == MODES).astype(F32)
            first = dot_nn(rows[begin:end, :], hot_a[:, span])
            second = dot_nn(rows[begin:end, :], hot_b[:, span]) + constant
            library[begin:end, span] = (first * second).astype(BF16)

    build(0, SLAB)
    square[...] = jnp.zeros_like(square)
    for step in (1, 3, 2):
        drain(rows.at[pl.ds(0, SLAB)], recv_sem.at[SLABS + step - 1])
    build(SLAB, LOCAL)

    drain(compact_in.at[pl.ds(0, (NX - 1) * ROWS)], recv_sem.at[COMPACT])
    given = jnp.concatenate([compact_in[k * ROWS : (k + 1) * ROWS, :] for k in range(NX)], axis=1)
    line, lane = iota((LOCAL, OWN), 0), iota((LOCAL, OWN), 1)
    from_x = lax.rem(x - line // 128 + NX, NX)
    pick = (
        (from_x * NY + line % 128 // 16 == lane // 8)
        & (line % 16 // 8 == y // 4)
        & (line % 8 == lane % 8)
    )
    mask = dot_nn(given, chosen(pick))[GROUP:]

    own_half = pl.ds(pl.multiple_of(core * HALF, HALF), HALF)
    their_half = pl.ds(pl.multiple_of((1 - core) * HALF, HALF), HALF)
    own_terms = pl.ds(pl.multiple_of(core * HALF + z * OWN, OWN), OWN)
    own_slice = pl.ds(pl.multiple_of(z * OWN, OWN), OWN)

    def scatter_sums(lhs, finish, out, pair, pre, got, at):
        out[...] = finish(dot_nn(lhs, library[:, their_half]))
        send(out, pair, PAIR + at, sibling)
        own = finish(dot_nn(lhs, library[:, own_half]))
        drain(pair, recv_sem.at[PAIR + at])
        pre[...] = own + pair[...]
        for step in FAR_FIRST:
            other, device = at_line(step)
            theirs = pl.ds(pl.multiple_of(other * OWN, OWN), OWN)
            send(pre.at[:, theirs], got.at[step - 1], SUMS + at, device)

    def sum_up(pre, got, at):
        drain(got, recv_sem.at[SUMS + at])
        total = pre[:, own_slice]
        for step in range(1, NZ):
            total = total + got[step - 1]
        return total * mask * (1.0 / SNAPS)

    def gather_slices(value, full, at):
        full[:, own_terms] = value
        for step in FAR_FIRST:
            send(full.at[:, own_terms], full.at[:, own_terms], SLICES + at, at_line(step)[1])
        drain(full.at[:, pl.ds(0, HALF - OWN)], recv_sem.at[SLICES + at])
        send(full.at[:, own_half], full.at[:, own_half], HALVES + at, sibling)

    def gather_halves(full, at):
        drain(full.at[:, pl.ds(0, HALF)], recv_sem.at[HALVES + at])

    def squares(vector):
        return jnp.sum(vector * vector, axis=1, keepdims=True)

    scatter_sums(given, lambda value: value[:GROUP], out0, pair0, pre0, got0, 0)
    direction = sum_up(pre0, got0, 0)
    gather_slices(direction, full0, 0)
    image = dot_nt(split(full0[:, own_half]), library[:, own_half])
    gather_halves(full0, 0)
    image = merge(image + dot_nt(split(full0[:, their_half]), library[:, their_half]))
    scatter_sums(split(image), merge, out1, pair1, pre1, got1, 1)
    whole = full0[...]
    energy = squares(whole)
    product = sum_up(pre1, got1, 1)
    gather_slices(product, full1, 1)
    gather_halves(full1, 1)
    whole_product = full1[...]
    step_len = energy / jnp.sum(whole * whole_product, axis=1, keepdims=True)
    whole_resid = whole - step_len * whole_product
    fresh = squares(whole_resid)
    ratio = fresh / energy
    coeffs = step_len * direction
    resid = direction - step_len * product
    direction = resid + ratio * direction
    image = merge(dot_nt(split(whole_resid + ratio * whole), library[...]))

    curve[0] = jnp.broadcast_to(squares(image), (GROUP, 128))
    send(curve.at[0], curve.at[1], CURVE, sibling)
    scatter_sums(split(image), merge, out2, pair2, pre2, got2, 2)
    drain(curve.at[1], recv_sem.at[CURVE])
    curve[2] = curve[0] + curve[1]
    for step in FAR_FIRST:
        send(curve.at[2], curves.at[step - 1], STAGES, at_line(step)[1])
    drain(curves, recv_sem.at[STAGES])
    total = curve[2]
    for step in range(1, NZ):
        total = total + curves[step - 1]
    product = sum_up(pre2, got2, 2)
    step_len = fresh / (total[:, 0:1] * (1.0 / SNAPS))
    coeffs = coeffs + step_len * direction
    resid = resid - step_len * product

    group = NX * y + x
    at = group % (PLANE // 2) * GROUP
    square[pl.ds(pl.multiple_of(at, GROUP), GROUP), :] = coeffs
    square[pl.ds(pl.multiple_of(lax.rem(at + 64, 128), GROUP), GROUP), :] = resid
    turn[...] = square[...].T
    here = pl.ds(pl.multiple_of((x * NY + y) * 8, 8), 8)
    for a, b in sorted(peers, key=lambda peer: -min(peer[0], NX - peer[0]) - min(peer[1], NY - peer[1])):
        spot = lax.rem(x + a, NX) * NY + lax.rem(y + b, NY)
        theirs = pl.ds(pl.multiple_of(spot * 8, 8), 8)
        send(turn.at[theirs], turned.at[here], TURN, at_plane(a, b))
    turned[here, :] = turn[here, :]
    drain(turned.at[pl.ds(0, OWN - 8)], recv_sem.at[TURN])
    lane = iota((8, 128), 1) // GROUP
    for side in range(2):
        left = jnp.zeros((8, 128), F32)
        right = left
        for a in range(NX):
            for b in range(4 * side, 4 * side + 4):
                block = turned[8 * (a * NY + b) : 8 * (a * NY + b) + 8, :]
                at = (NX * b + a) % (PLANE // 2)
                left = jnp.where(lane == at, block, left)
                right = jnp.where(lane == (at + 8) % 16, block, right)
        out_ref[0:8, 128 * side : 128 * side + 128] = left
        out_ref[8:16, 128 * side : 128 * side + 128] = pltpu.roll(right, 64, 1)

    drain(rows.at[pl.ds(0, (NY - 1) * ROWS)], send_sem.at[0])
    drain(extra.at[pl.ds(0, (NY - 1) * ROWS)], send_sem.at[EXTRA])
    for step in (1, 2, 3):
        drain(rows.at[pl.ds(0, SLAB)], send_sem.at[SLABS + step - 1])
    drain(compact_in.at[pl.ds(0, (NX - 1) * ROWS)], send_sem.at[COMPACT])
    for k, (pair, got) in enumerate(((pair0, got0), (pair1, got1), (pair2, got2))):
        drain(pair, send_sem.at[PAIR + k])
        drain(got, send_sem.at[SUMS + k])
    for k, full in enumerate((full0, full1)):
        drain(full.at[:, pl.ds(0, HALF - OWN)], send_sem.at[SLICES + k])
        drain(full.at[:, pl.ds(0, HALF)], send_sem.at[HALVES + k])
    drain(curve.at[1], send_sem.at[CURVE])
    drain(curves, send_sem.at[STAGES])
    drain(turned.at[pl.ds(0, OWN - 8)], send_sem.at[TURN])


def body(modes, targets, pairs, support):
    vmem = pl.BlockSpec(memory_space=pltpu.VMEM)
    hbm = pl.BlockSpec(memory_space=pltpu.HBM)
    both = pl.pallas_call(
        kernel,
        out_shape=jax.ShapeDtypeStruct((16, TARGETS), F32),
        in_specs=[hbm] * 4,
        out_specs=vmem,
        scratch_shapes=[
            pltpu.VMEM((ROWS, TARGETS), BF16),
            pltpu.VMEM((2, TERMS), jnp.int32),
            pltpu.VMEM((8, TARGETS), jnp.int32),
            pltpu.VMEM((LOCAL, MODES), BF16),
            pltpu.VMEM((SLAB, TARGETS + 128), BF16),
            pltpu.VMEM((NX * ROWS, 128), BF16),
            pltpu.VMEM((NX * ROWS, 128), BF16),
            pltpu.VMEM((MODES, TERMS), BF16),
            pltpu.VMEM((MODES, TERMS), BF16),
            pltpu.VMEM((2 * NZ, 512), jnp.int32),
            pltpu.VMEM((LOCAL, TERMS), BF16),
        ]
        + [pltpu.VMEM((GROUP, HALF), F32)] * 9
        + [pltpu.VMEM((NZ - 1, GROUP, OWN), F32)] * 3
        + [pltpu.VMEM((GROUP, TERMS), F32)] * 2
        + [
            pltpu.VMEM((3, GROUP, 128), F32),
            pltpu.VMEM((NZ - 1, GROUP, 128), F32),
            pltpu.VMEM((OWN, 128), F32),
            pltpu.VMEM((128, OWN), F32),
            pltpu.VMEM((OWN, 128), F32),
            pltpu.SemaphoreType.DMA((4,)),
            pltpu.SemaphoreType.DMA((STAGES + 1,)),
            pltpu.SemaphoreType.DMA((STAGES + 1,)),
        ],
        compiler_params=pltpu.CompilerParams(
            collective_id=0, has_side_effects=True, vmem_limit_bytes=64 * 2**20
        ),
        name="regression",
    )(modes, targets, pairs.T, support)
    return both[:8], both[8:]


def solution(mesh):
    rows = P(("snap", "tile"), None)
    return jax.shard_map(
        body,
        mesh=mesh,
        in_specs=(rows, rows, P(), rows),
        out_specs=(rows, rows),
        check_vma=False,
    )
```

time: 835 us -> 68.1 us (0.08)
  blocking collectives: 390 us -> 0 us
  waiting for transfers between devices: 317 us -> 0 us
  local copies, waits for them, and re-layouts: 76.7 us -> 1.32 us
  Pallas kernels: 0 us -> 65.6 us
  other arithmetic: 21.2 us -> 0 us
  matrix products: 15.7 us -> 0 us
  between operations: 13.8 us -> 0.64 us
    psum x3 -> x0, blocking collectives: 286 us -> none  [the longest x2 190 us: energy_of(): return lax.psum(jnp.sum(vector * vector, axis=0), ('snap', 'tile'))]
    all_gather x2 -> x0, waiting for transfers between devices: 239 us -> none  [body(): lax.all_gather(direction, ('snap', 'tile'), axis=0, tiled=True)]
    all_gather x2 -> x0, blocking collectives: 104 us -> none  [the longest x1 54.4 us: body(): rows_in = lax.all_gather(modes, 'tile', axis=0, tiled=True)]
    psum x1 -> x0, waiting for transfers between devices: 77.7 us -> none  [body(): gram_all, cross_all = lax.psum((gram_part, cross_part), 'snap')]
    gather x6 -> x0, local copies, waits for them, and re-layouts: 74.4 us -> none  [the longest x2 33.8 us: inner(): jnp.take(extended, first_factor, axis=1)]
    pallas_call x0 -> x1, Pallas kernels: none -> 65.6 us  [body(): pl.pallas_call(kernel, out_shape=jax.ShapeDtypeStruct((16, TARGETS), F32)...]
    convert_element_type x2 -> x0, other arithmetic: 18.4 us -> none  [inner(): library = (jnp.take(extended, first_factor, axis=1) * jnp.take(extended,...]
    dot_general x6 -> x0, matrix products: 15.7 us -> none  [the longest x2 7.87 us: body(): jnp.dot(gram_rows, lax.all_gather(direction, ('snap', 'tile'), axis=0, ti...]
  transfers between devices with their start and end apart: 3 -> 0, of which waited for: 3 -> 0; matrix products, arithmetic and copies ran while one was open for 0% -> 0% of each run, Pallas kernels for 0% -> 0%
where the time goes in v2:
time: 68.1 us; the launch traced here: 67.6 us
  Pallas kernels  65.6 us (96%)
  local copies, waits for them, and re-layouts  1.32 us (2%)
    pallas_call x1, Pallas kernels, body(): pl.pallas_call(kernel, out_shape=jax.ShapeDtypeStruct((16, TARGETS), F32)...  65.6 us

profile of v2, /device:TPU:1, one launch (start us, length us, event | category | flops | bytes accessed | tf_op | source)
XLA Modules:
  0.0 67.6 jit_solution(4667197151203088055)
XLA Ops:
  0.6 65.6 %regression.1 = f32[16,256]{1,0:T(8,128)} custom-call(bf16[16,256]{1,0:T(8,128)(2,1)} %modes_ref.1, bf16[16,256]{1,0:T(8,128)(2,1)} %targets_ref.1, s32[2,4096]{1,0:T(2,128)} %bitcast.1, s32[8,256]{1,0:T(8,128)} %support_ref.1), custom_call_target="tpu_custom_call" | custom-call | tf_op jit(solution)/shard_map/regression/pallas_call | solution.py:328
  66.3 1.3 %fusion = (f32[8,256]{1,0:T(8,128)}, f32[8,256]{1,0:T(8,128)}) fusion(f32[16,256]{1,0:T(8,128)} %regression.1), kind=kLoop, calls=%fused_computation | loop fusion | bytes 32768 | tf_op jit(solution)/shard_map/slice | solution.py:364

commit v3 on v2

--- a/solution.py
+++ b/solution.py
@@ -25,8 +25,9 @@
 BF16 = jnp.bfloat16
 MESH = pl.DeviceIdType.MESH
 
-EXTRA, SLABS, COMPACT, PAIR, SUMS, SLICES, HALVES, CURVE, TURN = 7, 8, 11, 12, 15, 18, 20, 22, 23
-STAGES = 24
+EXTRA, SLABS, COMPACT, PAIR, SUMS, SLICES, HALVES, CURVE, CURVES, TURN = 7, 8, 11, 12, 15, 18, 20, 22, 24, 26
+ARRIVED = 27
+STAGES = ARRIVED + 2 * RING
 
 
 def split(value):
@@ -64,7 +65,7 @@
     targets_in, pairs_in, support_in, rows, extra, compact, compact_in,
     hot_a, hot_b, terms, library,
     out0, out1, out2, pair0, pair1, pair2, pre0, pre1, pre2, got0, got1, got2,
-    full0, full1, curve, curves, turn, square, turned,
+    full0, full1, curve1, curve2, curves1, curves2, turn, square, turned,
     load_sem, send_sem, recv_sem,
 ):
     z = lax.axis_index("snap")
@@ -154,7 +155,6 @@
     for step in NEAR_FIRST:
         drain(rows.at[pl.ds(0, ROWS)], recv_sem.at[step - 1])
         forward(lax.rem(y - step + NY, NY))
-    make_hot(1)
 
     drain(extra.at[pl.ds(0, (NY - 1) * ROWS)], recv_sem.at[EXTRA])
     line = iota((NX * ROWS, TARGETS), 0)
@@ -174,6 +174,8 @@
         )
     compact_in[0:ROWS, :] = compact[pl.ds(pl.multiple_of(x * ROWS, ROWS), ROWS), :]
 
+    make_hot(1)
+
     def build(begin, end):
         for k in range(TERMS // CHUNK):
             span = slice(k * CHUNK, (k + 1) * CHUNK)
@@ -198,6 +200,105 @@
 
     drain(compact_in.at[pl.ds(0, (NX - 1) * ROWS)], recv_sem.at[COMPACT])
     given = jnp.concatenate([compact_in[k * ROWS : (k + 1) * ROWS, :] for k in range(NX)], axis=1)
+    own_half = pl.ds(pl.multiple_of(core * HALF, HALF), HALF)
+    their_half = pl.ds(pl.multiple_of((1 - core) * HALF, HALF), HALF)
+    own_terms = pl.ds(pl.multiple_of(core * HALF + z * OWN, OWN), OWN)
+    own_slice = pl.ds(pl.multiple_of(z * OWN, OWN), OWN)
+
+    def squares(vector):
+        return jnp.sum(vector * vector, axis=1, keepdims=True)
+
+    diagonal = iota((GROUP, 128), 0) == iota((GROUP, 128), 1)
+
+    def to_row(column):
+        return jnp.sum(jnp.where(diagonal, column, 0.0), axis=0, keepdims=True)
+
+    def to_column(row):
+        return jnp.sum(jnp.where(diagonal, row, 0.0), axis=1, keepdims=True)
+
+    def scatter_sums(lhs, finish, out, pair, pre, got, at, image=None, curve=None, curves=None):
+        if image is not None:
+            curve[0] = to_row(squares(image))
+            send(curve.at[0], curve.at[1], CURVE + at - 1, sibling)
+        out[...] = finish(dot_nn(lhs, library[:, their_half]))
+        send(out, pair, PAIR + at, sibling)
+        own = finish(dot_nn(lhs, library[:, own_half]))
+        if image is not None:
+            drain(curve.at[1], recv_sem.at[CURVE + at - 1])
+            curve[2] = curve[0] + curve[1]
+        drain(pair, recv_sem.at[PAIR + at])
+        pre[...] = own + pair[...]
+        for step in FAR_FIRST:
+            other, device = at_line(step)
+            theirs = pl.ds(pl.multiple_of(other * OWN, OWN), OWN)
+            send(pre.at[:, theirs], got.at[step - 1], SUMS + at, device)
+            if image is not None:
+                send(curve.at[2], curves.at[step - 1], CURVES + at - 1, device)
+
+    def sum_up(pre, got, at):
+        drain(got, recv_sem.at[SUMS + at])
+        total = pre[:, own_slice]
+        for step in range(1, NZ):
+            total = total + got[step - 1]
+        return total * mask * (1.0 / SNAPS)
+
+    def curvature(curve, curves, at):
+        drain(curves, recv_sem.at[CURVES + at - 1])
+        total = curve[2]
+        for step in range(1, NZ):
+            total = total + curves[step - 1]
+        return to_column(total) * (1.0 / SNAPS)
+
+    def gather_terms(value, full, at):
+        arrived = ARRIVED + RING * at
+
+        def slice_of(side, step):
+            begin = side * HALF + lax.rem(z - step + NZ, NZ) * OWN
+            return full.at[:, pl.ds(pl.multiple_of(begin, OWN), OWN)]
+
+        def forward(step):
+            send(slice_of(core, step), slice_of(core, step), HALVES + at, sibling, arrived + NZ + step)
+
+        def wait(side, steps):
+            for step in steps:
+                slot = arrived + step if side == 0 else arrived + NZ + step
+                drain(full.at[:, pl.ds(0, OWN)], recv_sem.at[slot])
+                if side == 0:
+                    forward(step)
+
+        def product(side, steps):
+            total = None
+            for step in steps:
+                which = core if side == 0 else 1 - core
+                begin = which * HALF + lax.rem(z - step + NZ, NZ) * OWN
+                span = pl.ds(pl.multiple_of(begin, OWN), OWN)
+                term = dot_nt(split(full[:, span]), library[:, span])
+                total = term if total is None else total + term
+            return total
+
+        full[:, own_terms] = value
+        for step in FAR_FIRST:
+            send(
+                slice_of(core, 0), slice_of(core, 0), SLICES + at, at_line(step)[1], arrived + step
+            )
+        forward(0)
+        wait(0, (1, 7))
+        image = product(0, (0, 1, 7))
+        wait(0, (2, 6))
+        wait(1, (0,))
+        image = image + product(0, (2, 6)) + product(1, (0,))
+        wait(0, (3, 5))
+        wait(1, (1, 7))
+        image = image + product(0, (3, 5)) + product(1, (1, 7))
+        wait(0, (4,))
+        wait(1, (2, 6))
+        image = image + product(0, (4,)) + product(1, (2, 6))
+        wait(1, (3, 5))
+        image = image + product(1, (3, 5))
+        wait(1, (4,))
+        return merge(image + product(1, (4,)))
+
+    scatter_sums(given, lambda value: value[:GROUP], out0, pair0, pre0, got0, 0)
     line, lane = iota((LOCAL, OWN), 0), iota((LOCAL, OWN), 1)
     from_x = lax.rem(x - line // 128 + NX, NX)
     pick = (
@@ -207,79 +308,22 @@
     )
     mask = dot_nn(given, chosen(pick))[GROUP:]
 
-    own_half = pl.ds(pl.multiple_of(core * HALF, HALF), HALF)
-    their_half = pl.ds(pl.multiple_of((1 - core) * HALF, HALF), HALF)
-    own_terms = pl.ds(pl.multiple_of(core * HALF + z * OWN, OWN), OWN)
-    own_slice = pl.ds(pl.multiple_of(z * OWN, OWN), OWN)
-
-    def scatter_sums(lhs, finish, out, pair, pre, got, at):
-        out[...] = finish(dot_nn(lhs, library[:, their_half]))
-        send(out, pair, PAIR + at, sibling)
-        own = finish(dot_nn(lhs, library[:, own_half]))
-        drain(pair, recv_sem.at[PAIR + at])
-        pre[...] = own + pair[...]
-        for step in FAR_FIRST:
-            other, device = at_line(step)
-            theirs = pl.ds(pl.multiple_of(other * OWN, OWN), OWN)
-            send(pre.at[:, theirs], got.at[step - 1], SUMS + at, device)
-
-    def sum_up(pre, got, at):
-        drain(got, recv_sem.at[SUMS + at])
-        total = pre[:, own_slice]
-        for step in range(1, NZ):
-            total = total + got[step - 1]
-        return total * mask * (1.0 / SNAPS)
-
-    def gather_slices(value, full, at):
-        full[:, own_terms] = value
-        for step in FAR_FIRST:
-            send(full.at[:, own_terms], full.at[:, own_terms], SLICES + at, at_line(step)[1])
-        drain(full.at[:, pl.ds(0, HALF - OWN)], recv_sem.at[SLICES + at])
-        send(full.at[:, own_half], full.at[:, own_half], HALVES + at, sibling)
-
-    def gather_halves(full, at):
-        drain(full.at[:, pl.ds(0, HALF)], recv_sem.at[HALVES + at])
-
-    def squares(vector):
-        return jnp.sum(vector * vector, axis=1, keepdims=True)
-
-    scatter_sums(given, lambda value: value[:GROUP], out0, pair0, pre0, got0, 0)
     direction = sum_up(pre0, got0, 0)
-    gather_slices(direction, full0, 0)
-    image = dot_nt(split(full0[:, own_half]), library[:, own_half])
-    gather_halves(full0, 0)
-    image = merge(image + dot_nt(split(full0[:, their_half]), library[:, their_half]))
-    scatter_sums(split(image), merge, out1, pair1, pre1, got1, 1)
-    whole = full0[...]
-    energy = squares(whole)
-    product = sum_up(pre1, got1, 1)
-    gather_slices(product, full1, 1)
-    gather_halves(full1, 1)
-    whole_product = full1[...]
-    step_len = energy / jnp.sum(whole * whole_product, axis=1, keepdims=True)
-    whole_resid = whole - step_len * whole_product
-    fresh = squares(whole_resid)
+    image = gather_terms(direction, full0, 0)
+    scatter_sums(split(image), merge, out1, pair1, pre1, got1, 1, image, curve1, curves1)
+    energy = squares(full0[...])
+    step_len = energy / curvature(curve1, curves1, 1)
+    coeffs = step_len * direction
+    resid = direction - step_len * sum_up(pre1, got1, 1)
+    next_image = gather_terms(resid, full1, 1)
+    fresh = squares(full1[...])
     ratio = fresh / energy
-    coeffs = step_len * direction
-    resid = direction - step_len * product
     direction = resid + ratio * direction
-    image = merge(dot_nt(split(whole_resid + ratio * whole), library[...]))
-
-    curve[0] = jnp.broadcast_to(squares(image), (GROUP, 128))
-    send(curve.at[0], curve.at[1], CURVE, sibling)
-    scatter_sums(split(image), merge, out2, pair2, pre2, got2, 2)
-    drain(curve.at[1], recv_sem.at[CURVE])
-    curve[2] = curve[0] + curve[1]
-    for step in FAR_FIRST:
-        send(curve.at[2], curves.at[step - 1], STAGES, at_line(step)[1])
-    drain(curves, recv_sem.at[STAGES])
-    total = curve[2]
-    for step in range(1, NZ):
-        total = total + curves[step - 1]
-    product = sum_up(pre2, got2, 2)
-    step_len = fresh / (total[:, 0:1] * (1.0 / SNAPS))
+    image = next_image + ratio * image
+    scatter_sums(split(image), merge, out2, pair2, pre2, got2, 2, image, curve2, curves2)
+    step_len = fresh / curvature(curve2, curves2, 2)
     coeffs = coeffs + step_len * direction
-    resid = resid - step_len * product
+    resid = resid - step_len * sum_up(pre2, got2, 2)
 
     group = NX * y + x
     at = group % (PLANE // 2) * GROUP
@@ -317,8 +361,9 @@
     for k, full in enumerate((full0, full1)):
         drain(full.at[:, pl.ds(0, HALF - OWN)], send_sem.at[SLICES + k])
         drain(full.at[:, pl.ds(0, HALF)], send_sem.at[HALVES + k])
-    drain(curve.at[1], send_sem.at[CURVE])
-    drain(curves, send_sem.at[STAGES])
+    for k, (curve, curves) in enumerate(((curve1, curves1), (curve2, curves2))):
+        drain(curve.at[1], send_sem.at[CURVE + k])
+        drain(curves, send_sem.at[CURVES + k])
     drain(turned.at[pl.ds(0, OWN - 8)], send_sem.at[TURN])
 
 
@@ -347,20 +392,22 @@
         + [pltpu.VMEM((NZ - 1, GROUP, OWN), F32)] * 3
         + [pltpu.VMEM((GROUP, TERMS), F32)] * 2
         + [
-            pltpu.VMEM((3, GROUP, 128), F32),
-            pltpu.VMEM((NZ - 1, GROUP, 128), F32),
+            pltpu.VMEM((3, 1, 128), F32),
+            pltpu.VMEM((3, 1, 128), F32),
+            pltpu.VMEM((NZ - 1, 1, 128), F32),
+            pltpu.VMEM((NZ - 1, 1, 128), F32),
             pltpu.VMEM((OWN, 128), F32),
             pltpu.VMEM((128, OWN), F32),
             pltpu.VMEM((OWN, 128), F32),
             pltpu.SemaphoreType.DMA((4,)),
-            pltpu.SemaphoreType.DMA((STAGES + 1,)),
-            pltpu.SemaphoreType.DMA((STAGES + 1,)),
+            pltpu.SemaphoreType.DMA((ARRIVED,)),
+            pltpu.SemaphoreType.DMA((STAGES,)),
         ],
         compiler_params=pltpu.CompilerParams(
-            collective_id=0, has_side_effects=True, vmem_limit_bytes=64 * 2**20
+            collective_id=0, has_side_effects=True, vmem_limit_bytes=48 * 2**20
         ),
         name="regression",
-    )(modes, targets, pairs.T, support)
+    )(*(pltpu.with_memory_space_constraint(v, pltpu.HBM) for v in (modes, targets, pairs.T, support)))
     return both[:8], both[8:]
 
 

time: 68.1 us -> 66 us (0.969)
  Pallas kernels: 65.6 us -> 64.6 us
  local copies, waits for them, and re-layouts: 1.32 us -> 0.61 us
    pallas_call x1, Pallas kernels: 65.6 us -> 64.6 us  [body(): pl.pallas_call(kernel, out_shape=jax.ShapeDtypeStruct((16, TARGETS), F32)...]
    slice x1, local copies, waits for them, and re-layouts: 1.32 us -> 0.61 us  [body(): return (both[:8], both[8:])]
where the time goes in v3:
time: 66 us; the launch traced here: 65.8 us
  Pallas kernels  64.6 us (98%)
    pallas_call x1, Pallas kernels, body(): pl.pallas_call(kernel, out_shape=jax.ShapeDtypeStruct((16, TARGETS), F32)...  64.6 us

profile of v3, /device:TPU:1, one launch (start us, length us, event | category | flops | bytes accessed | tf_op | source)
XLA Modules:
  0.0 65.8 jit_solution(5842922498470840412)
XLA Ops:
  0.6 64.6 %regression.1 = f32[16,256]{1,0:T(8,128)S(1)} custom-call(bf16[16,256]{1,0:T(8,128)(2,1)} %modes_ref.1, bf16[16,256]{1,0:T(8,128)(2,1)} %targets_ref.1, s32[2,4096]{1,0:T(2,128)} %bitcast.1, s32[8,256]{1,0:T(8,128)} %support_ref.1), custom_call_target="tpu_custom_call" | custom-call | tf_op jit(solution)/shard_map/regression/pallas_call | solution.py:373
  65.2 0.6 fusion

commit v4 on v3

--- a/solution.py
+++ b/solution.py
@@ -64,7 +64,7 @@
     modes_ref, targets_ref, pairs_ref, support_ref, out_ref,
     targets_in, pairs_in, support_in, rows, extra, compact, compact_in,
     hot_a, hot_b, terms, library,
-    out0, out1, out2, pair0, pair1, pair2, pre0, pre1, pre2, got0, got1, got2,
+    out0, out1, out2, mine0, mine1, mine2, pair0, pair1, pair2, pre0, pre1, pre2, got0, got1, got2,
     full0, full1, curve1, curve2, curves1, curves2, turn, square, turned,
     load_sem, send_sem, recv_sem,
 ):
@@ -82,6 +82,8 @@
         return other, (other, tile)
 
     sibling = (z, tile + 1 - 2 * core)
+    opposite = lax.rem(z + NZ // 2, NZ)
+    across = (opposite, tile + 1 - 2 * core)
 
     own_block = pl.ds(pl.multiple_of(y * ROWS, ROWS), ROWS)
     loads = [
@@ -100,6 +102,7 @@
     for step in range(1, NZ):
         pl.semaphore_signal(barrier, inc=1, device_id=at_line(step)[1], device_id_type=MESH)
     pl.semaphore_signal(barrier, inc=1, device_id=sibling, device_id_type=MESH)
+    pl.semaphore_signal(barrier, inc=1, device_id=across, device_id_type=MESH)
 
     def send(src, dst, stage, device, arrive=None):
         pltpu.make_async_remote_copy(
@@ -115,7 +118,7 @@
     extra[own_block, TARGETS:] = jnp.concatenate(
         [active[:, :128], active[:, 128:]], axis=0
     ).astype(BF16)
-    pl.semaphore_wait(barrier, len(peers) + NZ - 1 + 1)
+    pl.semaphore_wait(barrier, len(peers) + NZ - 1 + 2)
 
     for step in FAR_FIRST:
         send(rows.at[own_block], rows.at[own_block], 0, at_plane(0, step), step - 1)
@@ -216,30 +219,34 @@
     def to_column(row):
         return jnp.sum(jnp.where(diagonal, row, 0.0), axis=1, keepdims=True)
 
-    def scatter_sums(lhs, finish, out, pair, pre, got, at, image=None, curve=None, curves=None):
+    def scatter_sums(lhs, finish, out, mine, pair, pre, got, at, image=None, curve=None, curves=None):
         if image is not None:
             curve[0] = to_row(squares(image))
             send(curve.at[0], curve.at[1], CURVE + at - 1, sibling)
         out[...] = finish(dot_nn(lhs, library[:, their_half]))
         send(out, pair, PAIR + at, sibling)
-        own = finish(dot_nn(lhs, library[:, own_half]))
+        far = pl.ds(pl.multiple_of(opposite * OWN, OWN), OWN)
+        send(out.at[:, far], got.at[NZ - 1], SUMS + at, across)
+        mine[...] = finish(dot_nn(lhs, library[:, own_half]))
+        send(mine.at[:, far], got.at[NZ // 2 - 1], SUMS + at, at_line(NZ // 2)[1])
         if image is not None:
             drain(curve.at[1], recv_sem.at[CURVE + at - 1])
             curve[2] = curve[0] + curve[1]
         drain(pair, recv_sem.at[PAIR + at])
-        pre[...] = own + pair[...]
+        pre[...] = mine[...] + pair[...]
         for step in FAR_FIRST:
             other, device = at_line(step)
             theirs = pl.ds(pl.multiple_of(other * OWN, OWN), OWN)
-            send(pre.at[:, theirs], got.at[step - 1], SUMS + at, device)
+            if step != NZ // 2:
+                send(pre.at[:, theirs], got.at[step - 1], SUMS + at, device)
             if image is not None:
                 send(curve.at[2], curves.at[step - 1], CURVES + at - 1, device)
 
     def sum_up(pre, got, at):
         drain(got, recv_sem.at[SUMS + at])
         total = pre[:, own_slice]
-        for step in range(1, NZ):
-            total = total + got[step - 1]
+        for step in range(NZ):
+            total = total + got[step]
         return total * mask * (1.0 / SNAPS)
 
     def curvature(curve, curves, at):
@@ -263,7 +270,7 @@
             for step in steps:
                 slot = arrived + step if side == 0 else arrived + NZ + step
                 drain(full.at[:, pl.ds(0, OWN)], recv_sem.at[slot])
-                if side == 0:
+                if side == 0 and step != NZ // 2:
                     forward(step)
 
         def product(side, steps):
@@ -281,6 +288,8 @@
             send(
                 slice_of(core, 0), slice_of(core, 0), SLICES + at, at_line(step)[1], arrived + step
             )
+            if step == NZ // 2:
+                send(slice_of(core, 0), slice_of(core, 0), SLICES + at, across, arrived + NZ + step)
         forward(0)
         wait(0, (1, 7))
         image = product(0, (0, 1, 7))
@@ -290,15 +299,13 @@
         wait(0, (3, 5))
         wait(1, (1, 7))
         image = image + product(0, (3, 5)) + product(1, (1, 7))
+        wait(1, (2, 6))
+        image = image + product(1, (2, 6))
         wait(0, (4,))
-        wait(1, (2, 6))
-        image = image + product(0, (4,)) + product(1, (2, 6))
-        wait(1, (3, 5))
-        image = image + product(1, (3, 5))
-        wait(1, (4,))
-        return merge(image + product(1, (4,)))
-
-    scatter_sums(given, lambda value: value[:GROUP], out0, pair0, pre0, got0, 0)
+        wait(1, (4, 3, 5))
+        return merge(image + product(0, (4,)) + product(1, (4, 3, 5)))
+
+    scatter_sums(given, lambda value: value[:GROUP], out0, mine0, pair0, pre0, got0, 0)
     line, lane = iota((LOCAL, OWN), 0), iota((LOCAL, OWN), 1)
     from_x = lax.rem(x - line // 128 + NX, NX)
     pick = (
@@ -310,7 +317,7 @@
 
     direction = sum_up(pre0, got0, 0)
     image = gather_terms(direction, full0, 0)
-    scatter_sums(split(image), merge, out1, pair1, pre1, got1, 1, image, curve1, curves1)
+    scatter_sums(split(image), merge, out1, mine1, pair1, pre1, got1, 1, image, curve1, curves1)
     energy = squares(full0[...])
     step_len = energy / curvature(curve1, curves1, 1)
     coeffs = step_len * direction
@@ -320,7 +327,7 @@
     ratio = fresh / energy
     direction = resid + ratio * direction
     image = next_image + ratio * image
-    scatter_sums(split(image), merge, out2, pair2, pre2, got2, 2, image, curve2, curves2)
+    scatter_sums(split(image), merge, out2, mine2, pair2, pre2, got2, 2, image, curve2, curves2)
     step_len = fresh / curvature(curve2, curves2, 2)
     coeffs = coeffs + step_len * direction
     resid = resid - step_len * sum_up(pre2, got2, 2)
@@ -336,6 +343,20 @@
         theirs = pl.ds(pl.multiple_of(spot * 8, 8), 8)
         send(turn.at[theirs], turned.at[here], TURN, at_plane(a, b))
     turned[here, :] = turn[here, :]
+    drain(rows.at[pl.ds(0, (NY - 1) * ROWS)], send_sem.at[0])
+    drain(extra.at[pl.ds(0, (NY - 1) * ROWS)], send_sem.at[EXTRA])
+    for step in (1, 2, 3):
+        drain(rows.at[pl.ds(0, SLAB)], send_sem.at[SLABS + step - 1])
+    drain(compact_in.at[pl.ds(0, (NX - 1) * ROWS)], send_sem.at[COMPACT])
+    for k, (pair, got) in enumerate(((pair0, got0), (pair1, got1), (pair2, got2))):
+        drain(pair, send_sem.at[PAIR + k])
+        drain(got, send_sem.at[SUMS + k])
+    for k, full in enumerate((full0, full1)):
+        drain(full.at[:, pl.ds(0, HALF)], send_sem.at[SLICES + k])
+        drain(full.at[:, pl.ds(0, HALF - OWN)], send_sem.at[HALVES + k])
+    for k, (curve, curves) in enumerate(((curve1, curves1), (curve2, curves2))):
+        drain(curve.at[1], send_sem.at[CURVE + k])
+        drain(curves, send_sem.at[CURVES + k])
     drain(turned.at[pl.ds(0, OWN - 8)], recv_sem.at[TURN])
     lane = iota((8, 128), 1) // GROUP
     for side in range(2):
@@ -350,20 +371,6 @@
         out_ref[0:8, 128 * side : 128 * side + 128] = left
         out_ref[8:16, 128 * side : 128 * side + 128] = pltpu.roll(right, 64, 1)
 
-    drain(rows.at[pl.ds(0, (NY - 1) * ROWS)], send_sem.at[0])
-    drain(extra.at[pl.ds(0, (NY - 1) * ROWS)], send_sem.at[EXTRA])
-    for step in (1, 2, 3):
-        drain(rows.at[pl.ds(0, SLAB)], send_sem.at[SLABS + step - 1])
-    drain(compact_in.at[pl.ds(0, (NX - 1) * ROWS)], send_sem.at[COMPACT])
-    for k, (pair, got) in enumerate(((pair0, got0), (pair1, got1), (pair2, got2))):
-        drain(pair, send_sem.at[PAIR + k])
-        drain(got, send_sem.at[SUMS + k])
-    for k, full in enumerate((full0, full1)):
-        drain(full.at[:, pl.ds(0, HALF - OWN)], send_sem.at[SLICES + k])
-        drain(full.at[:, pl.ds(0, HALF)], send_sem.at[HALVES + k])
-    for k, (curve, curves) in enumerate(((curve1, curves1), (curve2, curves2))):
-        drain(curve.at[1], send_sem.at[CURVE + k])
-        drain(curves, send_sem.at[CURVES + k])
     drain(turned.at[pl.ds(0, OWN - 8)], send_sem.at[TURN])
 
 
@@ -388,8 +395,8 @@
             pltpu.VMEM((2 * NZ, 512), jnp.int32),
             pltpu.VMEM((LOCAL, TERMS), BF16),
         ]
-        + [pltpu.VMEM((GROUP, HALF), F32)] * 9
-        + [pltpu.VMEM((NZ - 1, GROUP, OWN), F32)] * 3
+        + [pltpu.VMEM((GROUP, HALF), F32)] * 12
+        + [pltpu.VMEM((NZ, GROUP, OWN), F32)] * 3
         + [pltpu.VMEM((GROUP, TERMS), F32)] * 2
         + [
             pltpu.VMEM((3, 1, 128), F32),

time: 66 us -> 64.4 us (0.976)
  Pallas kernels: 64.6 us -> 63 us
    pallas_call x1, Pallas kernels: 64.6 us -> 63 us  [body(): pl.pallas_call(kernel, out_shape=jax.ShapeDtypeStruct((16, TARGETS), F32)...]
where the time goes in v4:
time: 64.4 us; the launch traced here: 64.2 us
  Pallas kernels  63 us (98%)
    pallas_call x1, Pallas kernels, body(): pl.pallas_call(kernel, out_shape=jax.ShapeDtypeStruct((16, TARGETS), F32)...  63 us

profile of v4, /device:TPU:1, one launch (start us, length us, event | category | flops | bytes accessed | tf_op | source)
XLA Modules:
  0.0 64.2 jit_solution(9716423052114509852)
XLA Ops:
  0.6 63.0 %regression.1 = f32[16,256]{1,0:T(8,128)S(1)} custom-call(bf16[16,256]{1,0:T(8,128)(2,1)} %modes_ref.1, bf16[16,256]{1,0:T(8,128)(2,1)} %targets_ref.1, s32[2,4096]{1,0:T(2,128)} %bitcast.1, s32[8,256]{1,0:T(8,128)} %support_ref.1), custom_call_target="tpu_custom_call" | custom-call | tf_op jit(solution)/shard_map/regression/pallas_call | solution.py:380
  63.6 0.6 fusion

commit v5 on v4

--- a/solution.py
+++ b/solution.py
@@ -14,6 +14,8 @@
 ROWS = 16
 SNAPS = 8192
 SLAB = NY * ROWS
+BAND = NX * ROWS
+EARLY = 5 * BAND
 LOCAL = PLANE * ROWS
 OWN = TERMS // RING
 HALF = TERMS // NC
@@ -21,12 +23,13 @@
 CHUNK = 1024
 FAR_FIRST = (4, 3, 5, 2, 6, 1, 7)
 NEAR_FIRST = (1, 7, 2, 6, 3, 5, 4)
+BAND_OF = (0, 1, 3, 5, 7, 6, 4, 2)
 F32 = jnp.float32
 BF16 = jnp.bfloat16
 MESH = pl.DeviceIdType.MESH
 
-EXTRA, SLABS, COMPACT, PAIR, SUMS, SLICES, HALVES, CURVE, CURVES, TURN = 7, 8, 11, 12, 15, 18, 20, 22, 24, 26
-ARRIVED = 27
+BANDS, COMPACT, PAIR, SUMS, SLICES, HALVES, CURVE, CURVES, TURN = 7, 9, 10, 13, 16, 18, 20, 22, 24
+ARRIVED = 25
 STAGES = ARRIVED + 2 * RING
 
 
@@ -62,7 +65,7 @@
 
 def kernel(
     modes_ref, targets_ref, pairs_ref, support_ref, out_ref,
-    targets_in, pairs_in, support_in, rows, extra, compact, compact_in,
+    targets_in, pairs_in, support_in, rows, extra, compact, compact_in, reorder, pick_mask,
     hot_a, hot_b, terms, library,
     out0, out1, out2, mine0, mine1, mine2, pair0, pair1, pair2, pre0, pre1, pre2, got0, got1, got2,
     full0, full1, curve1, curve2, curves1, curves2, turn, square, turned,
@@ -87,7 +90,7 @@
 
     own_block = pl.ds(pl.multiple_of(y * ROWS, ROWS), ROWS)
     loads = [
-        pltpu.make_async_copy(modes_ref, rows.at[own_block], load_sem.at[0]),
+        pltpu.make_async_copy(modes_ref, rows.at[pl.ds(0, ROWS)], load_sem.at[0]),
         pltpu.make_async_copy(targets_ref, targets_in, load_sem.at[1]),
         pltpu.make_async_copy(support_ref, support_in, load_sem.at[2]),
         pltpu.make_async_copy(pairs_ref, pairs_in, load_sem.at[3]),
@@ -111,6 +114,10 @@
             device_id=device, device_id_type=MESH,
         ).start()
 
+    def block(step_y, step_x):
+        return rows.at[pl.ds(BAND_OF[step_y] * BAND + step_x * ROWS, ROWS)]
+
+    extra[...] = jnp.zeros_like(extra)
     for load in loads[:3]:
         load.wait()
     extra[own_block, 0:TARGETS] = targets_in[...]
@@ -121,22 +128,47 @@
     pl.semaphore_wait(barrier, len(peers) + NZ - 1 + 2)
 
     for step in FAR_FIRST:
-        send(rows.at[own_block], rows.at[own_block], 0, at_plane(0, step), step - 1)
-
-    def forward(block):
-        source = pl.multiple_of(block * ROWS, ROWS)
+        send(block(0, 0), block(step, 0), 0, at_plane(0, step), step - 1)
+
+    def forward(step_y):
         for step in (2, 1, 3):
-            target = pl.multiple_of(step * SLAB + block * ROWS, ROWS)
-            send(
-                rows.at[pl.ds(source, ROWS)], rows.at[pl.ds(target, ROWS)], SLABS + step - 1,
-                at_plane(step, 0),
-            )
-
-    forward(y)
-    for step in FAR_FIRST:
-        send(extra.at[own_block], extra.at[own_block], EXTRA, at_plane(0, step))
+            stage = BANDS + (BAND_OF[step_y] >= EARLY // BAND)
+            send(block(step_y, 0), block(step_y, step), stage, at_plane(step, 0))
+
+    def pass_on(steps):
+        for step in steps:
+            drain(rows.at[pl.ds(0, ROWS)], recv_sem.at[step - 1])
+            forward(step)
+
+    forward(0)
+
+    line = iota((PLANE * ROWS, TARGETS), 0)
+    ring = line // ROWS % NY * NX + line // (ROWS * NY)
+    pick_targets = chosen(
+        (iota((PLANE * ROWS, TARGETS), 1) == ring * GROUP + line % ROWS) & (line % ROWS < GROUP)
+    )
+    line = iota((PLANE * ROWS, 128), 0)
+    ring = (line // ROWS % NY * NX + line // (ROWS * NY)) % (PLANE // 2)
+    pick_flags = chosen(
+        (iota((PLANE * ROWS, 128), 1) == ring * GROUP + line % ROWS - GROUP) & (line % ROWS >= GROUP)
+    )
+    compact[...] = (
+        dot_nt(pick_targets, extra[:, 0:TARGETS]) + dot_nt(pick_flags, extra[:, TARGETS:])
+    ).astype(BF16)
+    far_first = sorted(peers, key=lambda peer: -min(peer[0], NX - peer[0]) - min(peer[1], NY - peer[1]))
+    for a, b in far_first:
+        spot = lax.rem(x + a, NX) * NY + lax.rem(y + b, NY)
+        send(
+            compact.at[pl.ds(pl.multiple_of(spot * ROWS, ROWS), ROWS)],
+            compact_in.at[pl.ds(pl.multiple_of((a * NY + y) * ROWS, ROWS), ROWS)],
+            COMPACT, at_plane(a, b),
+        )
+    compact_in[own_block, :] = compact[
+        pl.ds(pl.multiple_of((x * NY + y) * ROWS, ROWS), ROWS), :
+    ]
 
     loads[3].wait()
+    pass_on((1, 7))
     pairs = pairs_in[...].astype(F32)
     stacked = jnp.concatenate(
         [pairs[side : side + 1, 512 * k : 512 * k + 512] for side in (0, 1) for k in range(NZ)],
@@ -154,29 +186,9 @@
             hot_a[:, span] = chosen(index == terms[k : k + 1, from_lane])
             hot_b[:, span] = chosen(index == terms[NZ + k : NZ + k + 1, from_lane])
 
+    pass_on((2, 6))
     make_hot(0)
-    for step in NEAR_FIRST:
-        drain(rows.at[pl.ds(0, ROWS)], recv_sem.at[step - 1])
-        forward(lax.rem(y - step + NY, NY))
-
-    drain(extra.at[pl.ds(0, (NY - 1) * ROWS)], recv_sem.at[EXTRA])
-    line = iota((NX * ROWS, TARGETS), 0)
-    wanted = (NX * y + line // ROWS) * GROUP + line % ROWS
-    pick_targets = chosen((iota((NX * ROWS, TARGETS), 1) == wanted) & (line % ROWS < GROUP))
-    line = iota((NX * ROWS, 128), 0)
-    wanted = (NX * (y % 4) + line // ROWS) * GROUP + line % ROWS - GROUP
-    pick_flags = chosen((iota((NX * ROWS, 128), 1) == wanted) & (line % ROWS >= GROUP))
-    compact[...] = (
-        dot_nt(pick_targets, extra[:, 0:TARGETS]) + dot_nt(pick_flags, extra[:, TARGETS:])
-    ).astype(BF16)
-    for step in (2, 1, 3):
-        theirs = pl.ds(pl.multiple_of(lax.rem(x + step, NX) * ROWS, ROWS), ROWS)
-        send(
-            compact.at[theirs], compact_in.at[pl.ds(step * ROWS, ROWS)], COMPACT,
-            at_plane(step, 0),
-        )
-    compact_in[0:ROWS, :] = compact[pl.ds(pl.multiple_of(x * ROWS, ROWS), ROWS), :]
-
+    pass_on((3, 5, 4))
     make_hot(1)
 
     def build(begin, end):
@@ -195,14 +207,35 @@
             second = dot_nn(rows[begin:end, :], hot_b[:, span]) + constant
             library[begin:end, span] = (first * second).astype(BF16)
 
-    build(0, SLAB)
     square[...] = jnp.zeros_like(square)
-    for step in (1, 3, 2):
-        drain(rows.at[pl.ds(0, SLAB)], recv_sem.at[SLABS + step - 1])
-    build(SLAB, LOCAL)
-
-    drain(compact_in.at[pl.ds(0, (NX - 1) * ROWS)], recv_sem.at[COMPACT])
-    given = jnp.concatenate([compact_in[k * ROWS : (k + 1) * ROWS, :] for k in range(NX)], axis=1)
+    line, lane = iota((LOCAL, LOCAL), 0), iota((LOCAL, LOCAL), 1)
+    back = lax.rem(y - line % SLAB // ROWS + NY, NY)
+    band = jnp.where(back <= 4, 2 * back - 1, 16 - 2 * back)
+    band = jnp.where(back == 0, 0, band)
+    reorder[...] = chosen(band * BAND + line // SLAB * ROWS + line % ROWS == lane)
+    line, lane = iota((LOCAL, OWN), 0), iota((LOCAL, OWN), 1)
+    from_x = lax.rem(x - line // 128 + NX, NX)
+    pick_mask[...] = chosen(
+        (from_x * NY + line % 128 // 16 == lane // 8)
+        & (line % 16 // 8 == y // 4)
+        & (line % 8 == lane % 8)
+    )
+
+    drain(rows.at[pl.ds(0, EARLY // NX * (NX - 1))], recv_sem.at[BANDS])
+    build(0, EARLY)
+    drain(rows.at[pl.ds(0, (LOCAL - EARLY) // NX * (NX - 1))], recv_sem.at[BANDS + 1])
+    build(EARLY, LOCAL)
+
+    drain(compact_in.at[pl.ds(0, (PLANE - 1) * ROWS)], recv_sem.at[COMPACT])
+    slabs = []
+    for k in range(NX):
+        total = compact_in[k * SLAB : k * SLAB + ROWS, :]
+        for j in range(1, NY):
+            total = total + compact_in[k * SLAB + j * ROWS : k * SLAB + (j + 1) * ROWS, :]
+        slabs.append(total)
+    given = jnp.concatenate(slabs, axis=1)
+    wanted = dot_nn(given, reorder[...]).astype(BF16)
+
     own_half = pl.ds(pl.multiple_of(core * HALF, HALF), HALF)
     their_half = pl.ds(pl.multiple_of((1 - core) * HALF, HALF), HALF)
     own_terms = pl.ds(pl.multiple_of(core * HALF + z * OWN, OWN), OWN)
@@ -305,16 +338,8 @@
         wait(1, (4, 3, 5))
         return merge(image + product(0, (4,)) + product(1, (4, 3, 5)))
 
-    scatter_sums(given, lambda value: value[:GROUP], out0, mine0, pair0, pre0, got0, 0)
-    line, lane = iota((LOCAL, OWN), 0), iota((LOCAL, OWN), 1)
-    from_x = lax.rem(x - line // 128 + NX, NX)
-    pick = (
-        (from_x * NY + line % 128 // 16 == lane // 8)
-        & (line % 16 // 8 == y // 4)
-        & (line % 8 == lane % 8)
-    )
-    mask = dot_nn(given, chosen(pick))[GROUP:]
-
+    scatter_sums(wanted, lambda value: value[:GROUP], out0, mine0, pair0, pre0, got0, 0)
+    mask = dot_nn(given, pick_mask[...])[GROUP:]
     direction = sum_up(pre0, got0, 0)
     image = gather_terms(direction, full0, 0)
     scatter_sums(split(image), merge, out1, mine1, pair1, pre1, got1, 1, image, curve1, curves1)
@@ -338,16 +363,15 @@
     square[pl.ds(pl.multiple_of(lax.rem(at + 64, 128), GROUP), GROUP), :] = resid
     turn[...] = square[...].T
     here = pl.ds(pl.multiple_of((x * NY + y) * 8, 8), 8)
-    for a, b in sorted(peers, key=lambda peer: -min(peer[0], NX - peer[0]) - min(peer[1], NY - peer[1])):
+    for a, b in far_first:
         spot = lax.rem(x + a, NX) * NY + lax.rem(y + b, NY)
         theirs = pl.ds(pl.multiple_of(spot * 8, 8), 8)
         send(turn.at[theirs], turned.at[here], TURN, at_plane(a, b))
     turned[here, :] = turn[here, :]
     drain(rows.at[pl.ds(0, (NY - 1) * ROWS)], send_sem.at[0])
-    drain(extra.at[pl.ds(0, (NY - 1) * ROWS)], send_sem.at[EXTRA])
-    for step in (1, 2, 3):
-        drain(rows.at[pl.ds(0, SLAB)], send_sem.at[SLABS + step - 1])
-    drain(compact_in.at[pl.ds(0, (NX - 1) * ROWS)], send_sem.at[COMPACT])
+    drain(rows.at[pl.ds(0, EARLY // NX * (NX - 1))], send_sem.at[BANDS])
+    drain(rows.at[pl.ds(0, (LOCAL - EARLY) // NX * (NX - 1))], send_sem.at[BANDS + 1])
+    drain(compact_in.at[pl.ds(0, (PLANE - 1) * ROWS)], send_sem.at[COMPACT])
     for k, (pair, got) in enumerate(((pair0, got0), (pair1, got1), (pair2, got2))):
         drain(pair, send_sem.at[PAIR + k])
         drain(got, send_sem.at[SUMS + k])
@@ -388,8 +412,10 @@
             pltpu.VMEM((8, TARGETS), jnp.int32),
             pltpu.VMEM((LOCAL, MODES), BF16),
             pltpu.VMEM((SLAB, TARGETS + 128), BF16),
-            pltpu.VMEM((NX * ROWS, 128), BF16),
-            pltpu.VMEM((NX * ROWS, 128), BF16),
+            pltpu.VMEM((PLANE * ROWS, 128), BF16),
+            pltpu.VMEM((PLANE * ROWS, 128), BF16),
+            pltpu.VMEM((LOCAL, LOCAL), BF16),
+            pltpu.VMEM((LOCAL, OWN), BF16),
             pltpu.VMEM((MODES, TERMS), BF16),
             pltpu.VMEM((MODES, TERMS), BF16),
             pltpu.VMEM((2 * NZ, 512), jnp.int32),

time: 64.4 us -> 64.6 us (level)
  no operation moved by 1% of the time
where the time goes in v5:
time: 64.6 us; the launch traced here: 64.3 us
  Pallas kernels  63.1 us (98%)
    pallas_call x1, Pallas kernels, body(): pl.pallas_call(kernel, out_shape=jax.ShapeDtypeStruct((16, TARGETS), F32)...  63.1 us

profile of v5, /device:TPU:1, one launch (start us, length us, event | category | flops | bytes accessed | tf_op | source)
XLA Modules:
  0.0 64.3 jit_solution(1644648741714878899)
XLA Ops:
  0.6 63.1 %regression.1 = f32[16,256]{1,0:T(8,128)S(1)} custom-call(bf16[16,256]{1,0:T(8,128)(2,1)} %modes_ref.1, bf16[16,256]{1,0:T(8,128)(2,1)} %targets_ref.1, s32[2,4096]{1,0:T(2,128)} %bitcast.1, s32[8,256]{1,0:T(8,128)} %support_ref.1), custom_call_target="tpu_custom_call" | custom-call | tf_op jit(solution)/shard_map/regression/pallas_call | solution.py:404
  63.7 0.6 fusion

commit v6 on v5

--- a/solution.py
+++ b/solution.py
@@ -15,7 +15,7 @@
 SNAPS = 8192
 SLAB = NY * ROWS
 BAND = NX * ROWS
-EARLY = 5 * BAND
+BATCHES = (0, 3, 5, 7, 8)
 LOCAL = PLANE * ROWS
 OWN = TERMS // RING
 HALF = TERMS // NC
@@ -23,13 +23,14 @@
 CHUNK = 1024
 FAR_FIRST = (4, 3, 5, 2, 6, 1, 7)
 NEAR_FIRST = (1, 7, 2, 6, 3, 5, 4)
+DIRECT = (4, 3, 5)
 BAND_OF = (0, 1, 3, 5, 7, 6, 4, 2)
 F32 = jnp.float32
 BF16 = jnp.bfloat16
 MESH = pl.DeviceIdType.MESH
 
-BANDS, COMPACT, PAIR, SUMS, SLICES, HALVES, CURVE, CURVES, TURN = 7, 9, 10, 13, 16, 18, 20, 22, 24
-ARRIVED = 25
+BANDS, COMPACT, PAIR, SUMS, SLICES, HALVES, CURVE, CURVES, TURN = 7, 11, 12, 15, 18, 20, 22, 24, 26
+ARRIVED = 27
 STAGES = ARRIVED + 2 * RING
 
 
@@ -85,8 +86,10 @@
         return other, (other, tile)
 
     sibling = (z, tile + 1 - 2 * core)
-    opposite = lax.rem(z + NZ // 2, NZ)
-    across = (opposite, tile + 1 - 2 * core)
+
+    def across(step):
+        return lax.rem(z + step, NZ), tile + 1 - 2 * core
+
 
     own_block = pl.ds(pl.multiple_of(y * ROWS, ROWS), ROWS)
     loads = [
@@ -105,7 +108,8 @@
     for step in range(1, NZ):
         pl.semaphore_signal(barrier, inc=1, device_id=at_line(step)[1], device_id_type=MESH)
     pl.semaphore_signal(barrier, inc=1, device_id=sibling, device_id_type=MESH)
-    pl.semaphore_signal(barrier, inc=1, device_id=across, device_id_type=MESH)
+    for step in DIRECT:
+        pl.semaphore_signal(barrier, inc=1, device_id=across(step), device_id_type=MESH)
 
     def send(src, dst, stage, device, arrive=None):
         pltpu.make_async_remote_copy(
@@ -125,14 +129,14 @@
     extra[own_block, TARGETS:] = jnp.concatenate(
         [active[:, :128], active[:, 128:]], axis=0
     ).astype(BF16)
-    pl.semaphore_wait(barrier, len(peers) + NZ - 1 + 2)
+    pl.semaphore_wait(barrier, len(peers) + NZ - 1 + 1 + len(DIRECT))
 
     for step in FAR_FIRST:
-        send(block(0, 0), block(step, 0), 0, at_plane(0, step), step - 1)
+        send(modes_ref, block(step, 0), 0, at_plane(0, step), step - 1)
 
     def forward(step_y):
         for step in (2, 1, 3):
-            stage = BANDS + (BAND_OF[step_y] >= EARLY // BAND)
+            stage = BANDS + sum(BAND_OF[step_y] >= end for end in BATCHES[1:-1])
             send(block(step_y, 0), block(step_y, step), stage, at_plane(step, 0))
 
     def pass_on(steps):
@@ -156,19 +160,22 @@
         dot_nt(pick_targets, extra[:, 0:TARGETS]) + dot_nt(pick_flags, extra[:, TARGETS:])
     ).astype(BF16)
     far_first = sorted(peers, key=lambda peer: -min(peer[0], NX - peer[0]) - min(peer[1], NY - peer[1]))
-    for a, b in far_first:
-        spot = lax.rem(x + a, NX) * NY + lax.rem(y + b, NY)
-        send(
-            compact.at[pl.ds(pl.multiple_of(spot * ROWS, ROWS), ROWS)],
-            compact_in.at[pl.ds(pl.multiple_of((a * NY + y) * ROWS, ROWS), ROWS)],
-            COMPACT, at_plane(a, b),
-        )
+
+    def give(some):
+        for a, b in some:
+            spot = lax.rem(x + a, NX) * NY + lax.rem(y + b, NY)
+            send(
+                compact.at[pl.ds(pl.multiple_of(spot * ROWS, ROWS), ROWS)],
+                compact_in.at[pl.ds(pl.multiple_of((a * NY + y) * ROWS, ROWS), ROWS)],
+                COMPACT, at_plane(a, b),
+            )
+
     compact_in[own_block, :] = compact[
         pl.ds(pl.multiple_of((x * NY + y) * ROWS, ROWS), ROWS), :
     ]
 
     loads[3].wait()
-    pass_on((1, 7))
+    give(far_first[:8])
     pairs = pairs_in[...].astype(F32)
     stacked = jnp.concatenate(
         [pairs[side : side + 1, 512 * k : 512 * k + 512] for side in (0, 1) for k in range(NZ)],
@@ -186,9 +193,14 @@
             hot_a[:, span] = chosen(index == terms[k : k + 1, from_lane])
             hot_b[:, span] = chosen(index == terms[NZ + k : NZ + k + 1, from_lane])
 
+    pass_on((1, 7))
+    give(far_first[8:14])
     pass_on((2, 6))
+    give(far_first[14:20])
+    pass_on((3, 5))
+    give(far_first[20:])
+    pass_on((4,))
     make_hot(0)
-    pass_on((3, 5, 4))
     make_hot(1)
 
     def build(begin, end):
@@ -221,10 +233,10 @@
         & (line % 8 == lane % 8)
     )
 
-    drain(rows.at[pl.ds(0, EARLY // NX * (NX - 1))], recv_sem.at[BANDS])
-    build(0, EARLY)
-    drain(rows.at[pl.ds(0, (LOCAL - EARLY) // NX * (NX - 1))], recv_sem.at[BANDS + 1])
-    build(EARLY, LOCAL)
+    for k in range(len(BATCHES) - 1):
+        begin, end = BATCHES[k : k + 2]
+        drain(rows.at[pl.ds(0, (end - begin) * ROWS * (NX - 1))], recv_sem.at[BANDS + k])
+        build(begin * BAND, end * BAND)
 
     drain(compact_in.at[pl.ds(0, (PLANE - 1) * ROWS)], recv_sem.at[COMPACT])
     slabs = []
@@ -258,10 +270,14 @@
             send(curve.at[0], curve.at[1], CURVE + at - 1, sibling)
         out[...] = finish(dot_nn(lhs, library[:, their_half]))
         send(out, pair, PAIR + at, sibling)
-        far = pl.ds(pl.multiple_of(opposite * OWN, OWN), OWN)
-        send(out.at[:, far], got.at[NZ - 1], SUMS + at, across)
+        for k, step in enumerate(DIRECT):
+            far = pl.ds(pl.multiple_of(at_line(step)[0] * OWN, OWN), OWN)
+            send(out.at[:, far], got.at[NZ - 1 + k], SUMS + at, across(step))
         mine[...] = finish(dot_nn(lhs, library[:, own_half]))
-        send(mine.at[:, far], got.at[NZ // 2 - 1], SUMS + at, at_line(NZ // 2)[1])
+        for step in DIRECT:
+            other, device = at_line(step)
+            far = pl.ds(pl.multiple_of(other * OWN, OWN), OWN)
+            send(mine.at[:, far], got.at[step - 1], SUMS + at, device)
         if image is not None:
             drain(curve.at[1], recv_sem.at[CURVE + at - 1])
             curve[2] = curve[0] + curve[1]
@@ -270,7 +286,7 @@
         for step in FAR_FIRST:
             other, device = at_line(step)
             theirs = pl.ds(pl.multiple_of(other * OWN, OWN), OWN)
-            if step != NZ // 2:
+            if step not in DIRECT:
                 send(pre.at[:, theirs], got.at[step - 1], SUMS + at, device)
             if image is not None:
                 send(curve.at[2], curves.at[step - 1], CURVES + at - 1, device)
@@ -278,7 +294,7 @@
     def sum_up(pre, got, at):
         drain(got, recv_sem.at[SUMS + at])
         total = pre[:, own_slice]
-        for step in range(NZ):
+        for step in range(NZ - 1 + len(DIRECT)):
             total = total + got[step]
         return total * mask * (1.0 / SNAPS)
 
@@ -303,7 +319,7 @@
             for step in steps:
                 slot = arrived + step if side == 0 else arrived + NZ + step
                 drain(full.at[:, pl.ds(0, OWN)], recv_sem.at[slot])
-                if side == 0 and step != NZ // 2:
+                if side == 0 and step not in DIRECT:
                     forward(step)
 
         def product(side, steps):
@@ -321,22 +337,25 @@
             send(
                 slice_of(core, 0), slice_of(core, 0), SLICES + at, at_line(step)[1], arrived + step
             )
-            if step == NZ // 2:
-                send(slice_of(core, 0), slice_of(core, 0), SLICES + at, across, arrived + NZ + step)
+            if step in DIRECT:
+                send(
+                    slice_of(core, 0), slice_of(core, 0), SLICES + at, across(step), arrived + NZ + step
+                )
         forward(0)
+        image = product(0, (0,))
+        wait(1, (0,))
+        image = image + product(1, (0,))
         wait(0, (1, 7))
-        image = product(0, (0, 1, 7))
         wait(0, (2, 6))
-        wait(1, (0,))
-        image = image + product(0, (2, 6)) + product(1, (0,))
+        image = image + product(0, (1, 7, 2, 6))
         wait(0, (3, 5))
-        wait(1, (1, 7))
-        image = image + product(0, (3, 5)) + product(1, (1, 7))
-        wait(1, (2, 6))
-        image = image + product(1, (2, 6))
+        wait(1, (3, 5))
+        image = image + product(0, (3, 5)) + product(1, (3, 5))
+        wait(1, (1, 7, 2, 6))
+        image = image + product(1, (1, 7, 2, 6))
         wait(0, (4,))
-        wait(1, (4, 3, 5))
-        return merge(image + product(0, (4,)) + product(1, (4, 3, 5)))
+        wait(1, (4,))
+        return merge(image + product(0, (4,)) + product(1, (4,)))
 
     scatter_sums(wanted, lambda value: value[:GROUP], out0, mine0, pair0, pre0, got0, 0)
     mask = dot_nn(given, pick_mask[...])[GROUP:]
@@ -369,15 +388,16 @@
         send(turn.at[theirs], turned.at[here], TURN, at_plane(a, b))
     turned[here, :] = turn[here, :]
     drain(rows.at[pl.ds(0, (NY - 1) * ROWS)], send_sem.at[0])
-    drain(rows.at[pl.ds(0, EARLY // NX * (NX - 1))], send_sem.at[BANDS])
-    drain(rows.at[pl.ds(0, (LOCAL - EARLY) // NX * (NX - 1))], send_sem.at[BANDS + 1])
+    for k in range(len(BATCHES) - 1):
+        some = (BATCHES[k + 1] - BATCHES[k]) * ROWS * (NX - 1)
+        drain(rows.at[pl.ds(0, some)], send_sem.at[BANDS + k])
     drain(compact_in.at[pl.ds(0, (PLANE - 1) * ROWS)], send_sem.at[COMPACT])
     for k, (pair, got) in enumerate(((pair0, got0), (pair1, got1), (pair2, got2))):
         drain(pair, send_sem.at[PAIR + k])
         drain(got, send_sem.at[SUMS + k])
     for k, full in enumerate((full0, full1)):
-        drain(full.at[:, pl.ds(0, HALF)], send_sem.at[SLICES + k])
-        drain(full.at[:, pl.ds(0, HALF - OWN)], send_sem.at[HALVES + k])
+        drain(full.at[:, pl.ds(0, (NZ - 1 + len(DIRECT)) * OWN)], send_sem.at[SLICES + k])
+        drain(full.at[:, pl.ds(0, (NZ - len(DIRECT)) * OWN)], send_sem.at[HALVES + k])
     for k, (curve, curves) in enumerate(((curve1, curves1), (curve2, curves2))):
         drain(curve.at[1], send_sem.at[CURVE + k])
         drain(curves, send_sem.at[CURVES + k])
@@ -422,7 +442,7 @@
             pltpu.VMEM((LOCAL, TERMS), BF16),
         ]
         + [pltpu.VMEM((GROUP, HALF), F32)] * 12
-        + [pltpu.VMEM((NZ, GROUP, OWN), F32)] * 3
+        + [pltpu.VMEM((NZ - 1 + len(DIRECT), GROUP, OWN), F32)] * 3
         + [pltpu.VMEM((GROUP, TERMS), F32)] * 2
         + [
             pltpu.VMEM((3, 1, 128), F32),

time: 64.6 us -> 67.4 us (1.043)
  Pallas kernels: 63.1 us -> 66 us
    pallas_call x1, Pallas kernels: 63.1 us -> 66 us  [body(): pl.pallas_call(kernel, out_shape=jax.ShapeDtypeStruct((16, TARGETS), F32)...]
where the time goes in v6:
time: 67.4 us; the launch traced here: 67.2 us
  Pallas kernels  66 us (98%)
    pallas_call x1, Pallas kernels, body(): pl.pallas_call(kernel, out_shape=jax.ShapeDtypeStruct((16, TARGETS), F32)...  66 us

profile of v6, /device:TPU:1, one launch (start us, length us, event | category | flops | bytes accessed | tf_op | source)
XLA Modules:
  0.0 67.2 jit_solution(13722753104177302921)
XLA Ops:
  0.6 66.0 %regression.1 = f32[16,256]{1,0:T(8,128)S(1)} custom-call(bf16[16,256]{1,0:T(8,128)(2,1)} %modes_ref.1, bf16[16,256]{1,0:T(8,128)(2,1)} %targets_ref.1, s32[2,4096]{1,0:T(2,128)} %bitcast.1, s32[8,256]{1,0:T(8,128)} %support_ref.1), custom_call_target="tpu_custom_call" | custom-call | tf_op jit(solution)/shard_map/regression/pallas_call | solution.py:424
  66.6 0.6 fusion

commit v7 on v4

--- a/solution.py
+++ b/solution.py
@@ -65,7 +65,7 @@
     targets_in, pairs_in, support_in, rows, extra, compact, compact_in,
     hot_a, hot_b, terms, library,
     out0, out1, out2, mine0, mine1, mine2, pair0, pair1, pair2, pre0, pre1, pre2, got0, got1, got2,
-    full0, full1, curve1, curve2, curves1, curves2, turn, square, turned,
+    full0, full1, curve1, curve2, curves1, curves2, turn, square, turned, packed, unpacked, spread,
     load_sem, send_sem, recv_sem,
 ):
     z = lax.axis_index("snap")
@@ -97,7 +97,8 @@
 
     barrier = pltpu.get_barrier_semaphore()
     peers = [(a, b) for a in range(NX) for b in range(NY) if a or b]
-    for a, b in peers:
+    lines = [(a, b) for a, b in peers if not (a and b)]
+    for a, b in lines:
         pl.semaphore_signal(barrier, inc=1, device_id=at_plane(a, b), device_id_type=MESH)
     for step in range(1, NZ):
         pl.semaphore_signal(barrier, inc=1, device_id=at_line(step)[1], device_id_type=MESH)
@@ -118,7 +119,7 @@
     extra[own_block, TARGETS:] = jnp.concatenate(
         [active[:, :128], active[:, 128:]], axis=0
     ).astype(BF16)
-    pl.semaphore_wait(barrier, len(peers) + NZ - 1 + 2)
+    pl.semaphore_wait(barrier, len(lines) + NZ - 1 + 2)
 
     for step in FAR_FIRST:
         send(rows.at[own_block], rows.at[own_block], 0, at_plane(0, step), step - 1)
@@ -197,6 +198,10 @@
 
     build(0, SLAB)
     square[...] = jnp.zeros_like(square)
+    quarter = iota((8, 128), 1) // PLANE
+    line, lane = iota((TARGETS, TARGETS), 0), iota((TARGETS, TARGETS), 1)
+    ring = line % PLANE % NY * NX + line % PLANE // NY
+    spread[...] = chosen(ring * GROUP + line // PLANE == lane)
     for step in (1, 3, 2):
         drain(rows.at[pl.ds(0, SLAB)], recv_sem.at[SLABS + step - 1])
     build(SLAB, LOCAL)
@@ -332,17 +337,23 @@
     coeffs = coeffs + step_len * direction
     resid = resid - step_len * sum_up(pre2, got2, 2)
 
-    group = NX * y + x
-    at = group % (PLANE // 2) * GROUP
-    square[pl.ds(pl.multiple_of(at, GROUP), GROUP), :] = coeffs
-    square[pl.ds(pl.multiple_of(lax.rem(at + 64, 128), GROUP), GROUP), :] = resid
+    square[0:GROUP, :] = coeffs
+    square[GROUP : 2 * GROUP, :] = resid
     turn[...] = square[...].T
-    here = pl.ds(pl.multiple_of((x * NY + y) * 8, 8), 8)
-    for a, b in sorted(peers, key=lambda peer: -min(peer[0], NX - peer[0]) - min(peer[1], NY - peer[1])):
+    lane = iota((PLANE, 128), 1) // (2 * GROUP)
+    total = turn[pl.ds(0, PLANE, stride=8), :]
+    for k in range(1, 8):
+        total = jnp.where(
+            lane == k, pltpu.roll(turn[pl.ds(k, PLANE, stride=8), :], 2 * GROUP * k, 1), total
+        )
+    for k in range(PLANE):
+        packed[k] = total[k : k + 1]
+    here = x * NY + y
+    far_first = sorted(peers, key=lambda peer: -min(peer[0], NX - peer[0]) - min(peer[1], NY - peer[1]))
+    for a, b in far_first:
         spot = lax.rem(x + a, NX) * NY + lax.rem(y + b, NY)
-        theirs = pl.ds(pl.multiple_of(spot * 8, 8), 8)
-        send(turn.at[theirs], turned.at[here], TURN, at_plane(a, b))
-    turned[here, :] = turn[here, :]
+        send(packed.at[spot], unpacked.at[here], TURN, at_plane(a, b))
+    unpacked[here] = packed[here]
     drain(rows.at[pl.ds(0, (NY - 1) * ROWS)], send_sem.at[0])
     drain(extra.at[pl.ds(0, (NY - 1) * ROWS)], send_sem.at[EXTRA])
     for step in (1, 2, 3):
@@ -357,21 +368,30 @@
     for k, (curve, curves) in enumerate(((curve1, curves1), (curve2, curves2))):
         drain(curve.at[1], send_sem.at[CURVE + k])
         drain(curves, send_sem.at[CURVES + k])
-    drain(turned.at[pl.ds(0, OWN - 8)], recv_sem.at[TURN])
-    lane = iota((8, 128), 1) // GROUP
-    for side in range(2):
-        left = jnp.zeros((8, 128), F32)
-        right = left
-        for a in range(NX):
-            for b in range(4 * side, 4 * side + 4):
-                block = turned[8 * (a * NY + b) : 8 * (a * NY + b) + 8, :]
-                at = (NX * b + a) % (PLANE // 2)
-                left = jnp.where(lane == at, block, left)
-                right = jnp.where(lane == (at + 8) % 16, block, right)
-        out_ref[0:8, 128 * side : 128 * side + 128] = left
-        out_ref[8:16, 128 * side : 128 * side + 128] = pltpu.roll(right, 64, 1)
-
-    drain(turned.at[pl.ds(0, OWN - 8)], send_sem.at[TURN])
+    drain(unpacked.at[pl.ds(0, PLANE - 1)], recv_sem.at[TURN])
+    received = jnp.concatenate(
+        [unpacked[k] for k in range(PLANE)] + [jnp.zeros((128 - PLANE, 128), F32)], axis=0
+    )
+    turned[...] = received.T
+    sides = []
+    for out in range(2):
+        for part in range(2):
+            total = turned[pl.ds(out * GROUP + 4 * part, 8, stride=2 * GROUP), :]
+            for k in range(1, 4):
+                more = turned[pl.ds(out * GROUP + 4 * part + k, 8, stride=2 * GROUP), :]
+                total = jnp.where(quarter == k, pltpu.roll(more, PLANE * k, 1), total)
+            sides.append(total)
+    both = jnp.concatenate(
+        [jnp.concatenate(sides[0:2], axis=1), jnp.concatenate(sides[2:4], axis=1)], axis=0
+    )
+    high = both.astype(BF16)
+    rest = both - high.astype(F32)
+    middle = rest.astype(BF16)
+    low = (rest - middle.astype(F32)).astype(BF16)
+    moved = dot_nn(jnp.concatenate([high, middle, low], axis=0), spread[...])
+    out_ref[...] = moved[0:16] + moved[16:32] + moved[32:48]
+
+    drain(unpacked.at[pl.ds(0, PLANE - 1)], send_sem.at[TURN])
 
 
 def body(modes, targets, pairs, support):
@@ -405,7 +425,10 @@
             pltpu.VMEM((NZ - 1, 1, 128), F32),
             pltpu.VMEM((OWN, 128), F32),
             pltpu.VMEM((128, OWN), F32),
-            pltpu.VMEM((OWN, 128), F32),
+            pltpu.VMEM((128, 128), F32),
+            pltpu.VMEM((PLANE, 1, 128), F32),
+            pltpu.VMEM((PLANE, 1, 128), F32),
+            pltpu.VMEM((TARGETS, TARGETS), BF16),
             pltpu.SemaphoreType.DMA((4,)),
             pltpu.SemaphoreType.DMA((ARRIVED,)),
             pltpu.SemaphoreType.DMA((STAGES,)),

time: 64.4 us -> 62.9 us (0.977)
  Pallas kernels: 63 us -> 61.5 us
    pallas_call x1, Pallas kernels: 63 us -> 61.5 us  [body(): pl.pallas_call(kernel, out_shape=jax.ShapeDtypeStruct((16, TARGETS), F32)...]
where the time goes in v7:
time: 62.9 us; the launch traced here: 62.8 us
  Pallas kernels  61.5 us (98%)
  between operations  0.64 us (1%)
    pallas_call x1, Pallas kernels, body(): pl.pallas_call(kernel, out_shape=jax.ShapeDtypeStruct((16, TARGETS), F32)...  61.5 us

profile of v7, /device:TPU:1, one launch (start us, length us, event | category | flops | bytes accessed | tf_op | source)
XLA Modules:
  0.0 62.8 jit_solution(6109802189239957392)
XLA Ops:
  0.6 61.5 %regression.1 = f32[16,256]{1,0:T(8,128)S(1)} custom-call(bf16[16,256]{1,0:T(8,128)(2,1)} %modes_ref.1, bf16[16,256]{1,0:T(8,128)(2,1)} %targets_ref.1, s32[2,4096]{1,0:T(2,128)} %bitcast.1, s32[8,256]{1,0:T(8,128)} %support_ref.1), custom_call_target="tpu_custom_call" | custom-call | tf_op jit(solution)/shard_map/regression/pallas_call | solution.py:400
  62.2 0.6 fusion

commit v8 on v7

--- a/solution.py
+++ b/solution.py
@@ -18,7 +18,7 @@
 OWN = TERMS // RING
 HALF = TERMS // NC
 GROUP = TARGETS // PLANE
-CHUNK = 1024
+CHUNK = 2048
 FAR_FIRST = (4, 3, 5, 2, 6, 1, 7)
 NEAR_FIRST = (1, 7, 2, 6, 3, 5, 4)
 F32 = jnp.float32
@@ -62,7 +62,7 @@
 
 def kernel(
     modes_ref, targets_ref, pairs_ref, support_ref, out_ref,
-    targets_in, pairs_in, support_in, rows, extra, compact, compact_in,
+    targets_in, pairs_in, support_in, rows, leaving, extra, compact, compact_in,
     hot_a, hot_b, terms, library,
     out0, out1, out2, mine0, mine1, mine2, pair0, pair1, pair2, pre0, pre1, pre2, got0, got1, got2,
     full0, full1, curve1, curve2, curves1, curves2, turn, square, turned, packed, unpacked, spread,
@@ -114,11 +114,18 @@
 
     for load in loads[:3]:
         load.wait()
-    extra[own_block, 0:TARGETS] = targets_in[...]
+    given = targets_in[...].astype(F32)
     active = support_in[...].astype(F32)
-    extra[own_block, TARGETS:] = jnp.concatenate(
-        [active[:, :128], active[:, 128:]], axis=0
-    ).astype(BF16)
+    active = jnp.concatenate([active[:, :128], active[:, 128:]], axis=0)
+    lane = iota((ROWS, 128), 1)
+    for k in range(NY):
+        left = given[:, k // 4 * 128 : k // 4 * 128 + 128]
+        shift = 32 * (k % 4)
+        left = pltpu.roll(left, 128 - shift, 1) if shift else left
+        right = pltpu.roll(active, (160 - shift) % 128, 1) if shift != 32 else active
+        both = jnp.where(lane < 32, left, jnp.where(lane < 64, right, 0.0))
+        leaving[k * ROWS : (k + 1) * ROWS, :] = both.astype(BF16)
+    extra[own_block, :] = leaving[own_block, :]
     pl.semaphore_wait(barrier, len(lines) + NZ - 1 + 2)
 
     for step in FAR_FIRST:
@@ -135,7 +142,8 @@
 
     forward(y)
     for step in FAR_FIRST:
-        send(extra.at[own_block], extra.at[own_block], EXTRA, at_plane(0, step))
+        theirs = pl.ds(pl.multiple_of(lax.rem(y + step, NY) * ROWS, ROWS), ROWS)
+        send(leaving.at[theirs], extra.at[own_block], EXTRA, at_plane(0, step))
 
     loads[3].wait()
     pairs = pairs_in[...].astype(F32)
@@ -161,15 +169,9 @@
         forward(lax.rem(y - step + NY, NY))
 
     drain(extra.at[pl.ds(0, (NY - 1) * ROWS)], recv_sem.at[EXTRA])
-    line = iota((NX * ROWS, TARGETS), 0)
-    wanted = (NX * y + line // ROWS) * GROUP + line % ROWS
-    pick_targets = chosen((iota((NX * ROWS, TARGETS), 1) == wanted) & (line % ROWS < GROUP))
     line = iota((NX * ROWS, 128), 0)
-    wanted = (NX * (y % 4) + line // ROWS) * GROUP + line % ROWS - GROUP
-    pick_flags = chosen((iota((NX * ROWS, 128), 1) == wanted) & (line % ROWS >= GROUP))
-    compact[...] = (
-        dot_nt(pick_targets, extra[:, 0:TARGETS]) + dot_nt(pick_flags, extra[:, TARGETS:])
-    ).astype(BF16)
+    column = line // ROWS * GROUP + line % GROUP + jnp.where(line % ROWS < GROUP, 0, 32)
+    compact[...] = dot_nt(chosen(iota((NX * ROWS, 128), 1) == column), extra[...]).astype(BF16)
     for step in (2, 1, 3):
         theirs = pl.ds(pl.multiple_of(lax.rem(x + step, NX) * ROWS, ROWS), ROWS)
         send(
@@ -228,6 +230,8 @@
         if image is not None:
             curve[0] = to_row(squares(image))
             send(curve.at[0], curve.at[1], CURVE + at - 1, sibling)
+            send(curve.at[0], curves.at[NZ // 2 - 1], CURVES + at - 1, at_line(NZ // 2)[1])
+            send(curve.at[0], curves.at[NZ - 1], CURVES + at - 1, across)
         out[...] = finish(dot_nn(lhs, library[:, their_half]))
         send(out, pair, PAIR + at, sibling)
         far = pl.ds(pl.multiple_of(opposite * OWN, OWN), OWN)
@@ -242,8 +246,9 @@
         for step in FAR_FIRST:
             other, device = at_line(step)
             theirs = pl.ds(pl.multiple_of(other * OWN, OWN), OWN)
-            if step != NZ // 2:
-                send(pre.at[:, theirs], got.at[step - 1], SUMS + at, device)
+            if step == NZ // 2:
+                continue
+            send(pre.at[:, theirs], got.at[step - 1], SUMS + at, device)
             if image is not None:
                 send(curve.at[2], curves.at[step - 1], CURVES + at - 1, device)
 
@@ -257,8 +262,8 @@
     def curvature(curve, curves, at):
         drain(curves, recv_sem.at[CURVES + at - 1])
         total = curve[2]
-        for step in range(1, NZ):
-            total = total + curves[step - 1]
+        for step in range(NZ):
+            total = total + curves[step]
         return to_column(total) * (1.0 / SNAPS)
 
     def gather_terms(value, full, at):
@@ -296,19 +301,23 @@
             if step == NZ // 2:
                 send(slice_of(core, 0), slice_of(core, 0), SLICES + at, across, arrived + NZ + step)
         forward(0)
+        image = product(0, (0,))
+        wait(1, (0,))
+        image = image + product(1, (0,))
         wait(0, (1, 7))
-        image = product(0, (0, 1, 7))
+        image = image + product(0, (1, 7))
         wait(0, (2, 6))
-        wait(1, (0,))
-        image = image + product(0, (2, 6)) + product(1, (0,))
         wait(0, (3, 5))
+        image = image + product(0, (2, 6, 3, 5))
         wait(1, (1, 7))
-        image = image + product(0, (3, 5)) + product(1, (1, 7))
+        image = image + product(1, (1, 7))
+        wait(0, (4,))
+        wait(1, (4,))
+        image = image + product(0, (4,)) + product(1, (4,))
         wait(1, (2, 6))
         image = image + product(1, (2, 6))
-        wait(0, (4,))
-        wait(1, (4, 3, 5))
-        return merge(image + product(0, (4,)) + product(1, (4, 3, 5)))
+        wait(1, (3, 5))
+        return merge(image + product(1, (3, 5)))
 
     scatter_sums(given, lambda value: value[:GROUP], out0, mine0, pair0, pre0, got0, 0)
     line, lane = iota((LOCAL, OWN), 0), iota((LOCAL, OWN), 1)
@@ -407,7 +416,8 @@
             pltpu.VMEM((2, TERMS), jnp.int32),
             pltpu.VMEM((8, TARGETS), jnp.int32),
             pltpu.VMEM((LOCAL, MODES), BF16),
-            pltpu.VMEM((SLAB, TARGETS + 128), BF16),
+            pltpu.VMEM((SLAB, 128), BF16),
+            pltpu.VMEM((SLAB, 128), BF16),
             pltpu.VMEM((NX * ROWS, 128), BF16),
             pltpu.VMEM((NX * ROWS, 128), BF16),
             pltpu.VMEM((MODES, TERMS), BF16),
@@ -421,8 +431,8 @@
         + [
             pltpu.VMEM((3, 1, 128), F32),
             pltpu.VMEM((3, 1, 128), F32),
-            pltpu.VMEM((NZ - 1, 1, 128), F32),
-            pltpu.VMEM((NZ - 1, 1, 128), F32),
+            pltpu.VMEM((NZ, 1, 128), F32),
+            pltpu.VMEM((NZ, 1, 128), F32),
             pltpu.VMEM((OWN, 128), F32),
             pltpu.VMEM((128, OWN), F32),
             pltpu.VMEM((128, 128), F32),

time: 62.9 us -> 62 us (0.986)
  Pallas kernels: 61.5 us -> 60.5 us
    pallas_call x1, Pallas kernels: 61.5 us -> 60.5 us  [body(): pl.pallas_call(kernel, out_shape=jax.ShapeDtypeStruct((16, TARGETS), F32)...]
where the time goes in v8:
time: 62 us; the launch traced here: 61.7 us
  Pallas kernels  60.5 us (98%)
  between operations  0.64 us (1%)
    pallas_call x1, Pallas kernels, body(): pl.pallas_call(kernel, out_shape=jax.ShapeDtypeStruct((16, TARGETS), F32)...  60.5 us

profile of v8, /device:TPU:1, one launch (start us, length us, event | category | flops | bytes accessed | tf_op | source)
XLA Modules:
  0.0 61.7 jit_solution(6412897729850524823)
XLA Ops:
  0.6 60.5 %regression.1 = f32[16,256]{1,0:T(8,128)S(1)} custom-call(bf16[16,256]{1,0:T(8,128)(2,1)} %modes_ref.1, bf16[16,256]{1,0:T(8,128)(2,1)} %targets_ref.1, s32[2,4096]{1,0:T(2,128)} %bitcast.1, s32[8,256]{1,0:T(8,128)} %support_ref.1), custom_call_target="tpu_custom_call" | custom-call | tf_op jit(solution)/shard_map/regression/pallas_call | solution.py:409
  61.1 0.6 fusion

commit v9 on v8

--- a/solution.py
+++ b/solution.py
@@ -27,7 +27,8 @@
 
 EXTRA, SLABS, COMPACT, PAIR, SUMS, SLICES, HALVES, CURVE, CURVES, TURN = 7, 8, 11, 12, 15, 18, 20, 22, 24, 26
 ARRIVED = 27
-STAGES = ARRIVED + 2 * RING
+MIDDLE = ARRIVED + 2 * RING
+STAGES = MIDDLE + 3
 
 
 def split(value):
@@ -63,7 +64,7 @@
 def kernel(
     modes_ref, targets_ref, pairs_ref, support_ref, out_ref,
     targets_in, pairs_in, support_in, rows, leaving, extra, compact, compact_in,
-    hot_a, hot_b, terms, library,
+    hot_a, hot_b, constant, terms, library,
     out0, out1, out2, mine0, mine1, mine2, pair0, pair1, pair2, pre0, pre1, pre2, got0, got1, got2,
     full0, full1, curve1, curve2, curves1, curves2, turn, square, turned, packed, unpacked, spread,
     load_sem, send_sem, recv_sem,
@@ -157,11 +158,15 @@
     index = iota((MODES, OWN), 0)
 
     def make_hot(c):
+        side = jnp.where(core == c, 0, HALF)
         for k in range(NZ):
             from_lane = slice(OWN * c, OWN * c + OWN)
-            span = slice(HALF * c + OWN * k, HALF * c + OWN * k + OWN)
+            begin = side + OWN * lax.rem(k - z + NZ, NZ)
+            span = pl.ds(pl.multiple_of(begin, OWN), OWN)
+            second = terms[NZ + k : NZ + k + 1, from_lane]
             hot_a[:, span] = chosen(index == terms[k : k + 1, from_lane])
-            hot_b[:, span] = chosen(index == terms[NZ + k : NZ + k + 1, from_lane])
+            hot_b[:, span] = chosen(index == second)
+            constant[:, span] = (second == MODES).astype(F32)
 
     make_hot(0)
     for step in NEAR_FIRST:
@@ -185,17 +190,8 @@
     def build(begin, end):
         for k in range(TERMS // CHUNK):
             span = slice(k * CHUNK, (k + 1) * CHUNK)
-            c, first_z = k * CHUNK // HALF, k * CHUNK % HALF // OWN
-            constant = jnp.concatenate(
-                [
-                    terms[NZ + j : NZ + j + 1, OWN * c : OWN * c + OWN]
-                    for j in range(first_z, first_z + CHUNK // OWN)
-                ],
-                axis=1,
-            )
-            constant = (constant == MODES).astype(F32)
             first = dot_nn(rows[begin:end, :], hot_a[:, span])
-            second = dot_nn(rows[begin:end, :], hot_b[:, span]) + constant
+            second = dot_nn(rows[begin:end, :], hot_b[:, span]) + constant[:, span]
             library[begin:end, span] = (first * second).astype(BF16)
 
     build(0, SLAB)
@@ -210,11 +206,6 @@
 
     drain(compact_in.at[pl.ds(0, (NX - 1) * ROWS)], recv_sem.at[COMPACT])
     given = jnp.concatenate([compact_in[k * ROWS : (k + 1) * ROWS, :] for k in range(NX)], axis=1)
-    own_half = pl.ds(pl.multiple_of(core * HALF, HALF), HALF)
-    their_half = pl.ds(pl.multiple_of((1 - core) * HALF, HALF), HALF)
-    own_terms = pl.ds(pl.multiple_of(core * HALF + z * OWN, OWN), OWN)
-    own_slice = pl.ds(pl.multiple_of(z * OWN, OWN), OWN)
-
     def squares(vector):
         return jnp.sum(vector * vector, axis=1, keepdims=True)
 
@@ -232,29 +223,46 @@
             send(curve.at[0], curve.at[1], CURVE + at - 1, sibling)
             send(curve.at[0], curves.at[NZ // 2 - 1], CURVES + at - 1, at_line(NZ // 2)[1])
             send(curve.at[0], curves.at[NZ - 1], CURVES + at - 1, across)
-        out[...] = finish(dot_nn(lhs, library[:, their_half]))
-        send(out, pair, PAIR + at, sibling)
-        far = pl.ds(pl.multiple_of(opposite * OWN, OWN), OWN)
+        far = pl.ds(NZ // 2 * OWN, OWN)
+        middle, start, end = (slice(a * OWN, b * OWN) for a, b in ((3, 6), (0, 3), (6, 8)))
+
+        def partial(side, where):
+            columns = slice(side * HALF + where.start, side * HALF + where.stop)
+            return finish(dot_nn(lhs, library[:, columns]))
+
+        out[:, middle] = partial(1, middle)
+        send(out.at[:, middle], pair.at[:, middle], PAIR + at, sibling, MIDDLE + at)
         send(out.at[:, far], got.at[NZ - 1], SUMS + at, across)
-        mine[...] = finish(dot_nn(lhs, library[:, own_half]))
+        mine[:, middle] = partial(0, middle)
         send(mine.at[:, far], got.at[NZ // 2 - 1], SUMS + at, at_line(NZ // 2)[1])
+        for where in (start, end):
+            out[:, where] = partial(1, where)
+            send(out.at[:, where], pair.at[:, where], PAIR + at, sibling)
+        for where in (start, end):
+            mine[:, where] = partial(0, where)
+
+        def share(step):
+            device = at_line(step)[1]
+            send(pre.at[:, pl.ds(step * OWN, OWN)], got.at[step - 1], SUMS + at, device)
+            if image is not None:
+                send(curve.at[2], curves.at[step - 1], CURVES + at - 1, device)
+
         if image is not None:
             drain(curve.at[1], recv_sem.at[CURVE + at - 1])
             curve[2] = curve[0] + curve[1]
-        drain(pair, recv_sem.at[PAIR + at])
-        pre[...] = mine[...] + pair[...]
-        for step in FAR_FIRST:
-            other, device = at_line(step)
-            theirs = pl.ds(pl.multiple_of(other * OWN, OWN), OWN)
-            if step == NZ // 2:
-                continue
-            send(pre.at[:, theirs], got.at[step - 1], SUMS + at, device)
-            if image is not None:
-                send(curve.at[2], curves.at[step - 1], CURVES + at - 1, device)
+        drain(pair.at[:, middle], recv_sem.at[MIDDLE + at])
+        pre[:, middle] = mine[:, middle] + pair[:, middle]
+        share(3)
+        share(5)
+        drain(pair.at[:, pl.ds(0, 5 * OWN)], recv_sem.at[PAIR + at])
+        for where in (start, end):
+            pre[:, where] = mine[:, where] + pair[:, where]
+        for step in (2, 6, 1, 7):
+            share(step)
 
     def sum_up(pre, got, at):
         drain(got, recv_sem.at[SUMS + at])
-        total = pre[:, own_slice]
+        total = pre[:, :OWN]
         for step in range(NZ):
             total = total + got[step]
         return total * mask * (1.0 / SNAPS)
@@ -269,12 +277,14 @@
     def gather_terms(value, full, at):
         arrived = ARRIVED + RING * at
 
-        def slice_of(side, step):
-            begin = side * HALF + lax.rem(z - step + NZ, NZ) * OWN
-            return full.at[:, pl.ds(pl.multiple_of(begin, OWN), OWN)]
+        def span(side, step):
+            return pl.ds(side * HALF + (NZ - step) % NZ * OWN, OWN)
 
         def forward(step):
-            send(slice_of(core, step), slice_of(core, step), HALVES + at, sibling, arrived + NZ + step)
+            send(
+                full.at[:, span(0, step)], full.at[:, span(1, step)], HALVES + at, sibling,
+                arrived + NZ + step,
+            )
 
         def wait(side, steps):
             for step in steps:
@@ -286,20 +296,16 @@
         def product(side, steps):
             total = None
             for step in steps:
-                which = core if side == 0 else 1 - core
-                begin = which * HALF + lax.rem(z - step + NZ, NZ) * OWN
-                span = pl.ds(pl.multiple_of(begin, OWN), OWN)
-                term = dot_nt(split(full[:, span]), library[:, span])
+                term = dot_nt(split(full[:, span(side, step)]), library[:, span(side, step)])
                 total = term if total is None else total + term
             return total
 
-        full[:, own_terms] = value
+        full[:, :OWN] = value
+        mine = full.at[:, pl.ds(0, OWN)]
         for step in FAR_FIRST:
-            send(
-                slice_of(core, 0), slice_of(core, 0), SLICES + at, at_line(step)[1], arrived + step
-            )
+            send(mine, full.at[:, span(0, step)], SLICES + at, at_line(step)[1], arrived + step)
             if step == NZ // 2:
-                send(slice_of(core, 0), slice_of(core, 0), SLICES + at, across, arrived + NZ + step)
+                send(mine, full.at[:, span(1, step)], SLICES + at, across, arrived + NZ + step)
         forward(0)
         image = product(0, (0,))
         wait(1, (0,))
@@ -422,6 +428,7 @@
             pltpu.VMEM((NX * ROWS, 128), BF16),
             pltpu.VMEM((MODES, TERMS), BF16),
             pltpu.VMEM((MODES, TERMS), BF16),
+            pltpu.VMEM((1, TERMS), F32),
             pltpu.VMEM((2 * NZ, 512), jnp.int32),
             pltpu.VMEM((LOCAL, TERMS), BF16),
         ]

time: 62 us -> 61 us (0.984)
  Pallas kernels: 60.5 us -> 59.6 us
    pallas_call x1, Pallas kernels: 60.5 us -> 59.6 us  [body(): pl.pallas_call(kernel, out_shape=jax.ShapeDtypeStruct((16, TARGETS), F32)...]
where the time goes in v9:
time: 61 us; the launch traced here: 60.8 us
  Pallas kernels  59.6 us (98%)
  between operations  0.64 us (1%)
  local copies, waits for them, and re-layouts  0.61 us (1%)
    pallas_call x1, Pallas kernels, body(): pl.pallas_call(kernel, out_shape=jax.ShapeDtypeStruct((16, TARGETS), F32)...  59.6 us

profile of v9, /device:TPU:1, one launch (start us, length us, event | category | flops | bytes accessed | tf_op | source)
XLA Modules:
  0.0 60.8 jit_solution(1438747679401490800)
XLA Ops:
  0.6 59.6 %regression.1 = f32[16,256]{1,0:T(8,128)S(1)} custom-call(bf16[16,256]{1,0:T(8,128)(2,1)} %modes_ref.1, bf16[16,256]{1,0:T(8,128)(2,1)} %targets_ref.1, s32[2,4096]{1,0:T(2,128)} %bitcast.1, s32[8,256]{1,0:T(8,128)} %support_ref.1), custom_call_target="tpu_custom_call" | custom-call | tf_op jit(solution)/shard_map/regression/pallas_call | solution.py:415
  60.2 0.6 fusion

commit v10 on v9

--- a/solution.py
+++ b/solution.py
@@ -200,9 +200,11 @@
     line, lane = iota((TARGETS, TARGETS), 0), iota((TARGETS, TARGETS), 1)
     ring = line % PLANE % NY * NX + line % PLANE // NY
     spread[...] = chosen(ring * GROUP + line // PLANE == lane)
-    for step in (1, 3, 2):
+    drain(rows.at[pl.ds(0, SLAB)], recv_sem.at[SLABS])
+    build(SLAB, 2 * SLAB)
+    for step in (3, 2):
         drain(rows.at[pl.ds(0, SLAB)], recv_sem.at[SLABS + step - 1])
-    build(SLAB, LOCAL)
+    build(2 * SLAB, LOCAL)
 
     drain(compact_in.at[pl.ds(0, (NX - 1) * ROWS)], recv_sem.at[COMPACT])
     given = jnp.concatenate([compact_in[k * ROWS : (k + 1) * ROWS, :] for k in range(NX)], axis=1)

time: 61 us -> 60.9 us (level)
  no operation moved by 1% of the time
where the time goes in v10:
time: 60.9 us; the launch traced here: 60.5 us
  Pallas kernels  59.2 us (97%)
  between operations  0.64 us (1%)
  local copies, waits for them, and re-layouts  0.61 us (1%)
    pallas_call x1, Pallas kernels, body(): pl.pallas_call(kernel, out_shape=jax.ShapeDtypeStruct((16, TARGETS), F32)...  59.2 us

profile of v10, /device:TPU:1, one launch (start us, length us, event | category | flops | bytes accessed | tf_op | source)
XLA Modules:
  0.0 60.5 jit_solution(16077413495648445602)
XLA Ops:
  0.6 59.2 %regression.1 = f32[16,256]{1,0:T(8,128)S(1)} custom-call(bf16[16,256]{1,0:T(8,128)(2,1)} %modes_ref.1, bf16[16,256]{1,0:T(8,128)(2,1)} %targets_ref.1, s32[2,4096]{1,0:T(2,128)} %bitcast.1, s32[8,256]{1,0:T(8,128)} %support_ref.1), custom_call_target="tpu_custom_call" | custom-call | tf_op jit(solution)/shard_map/regression/pallas_call | solution.py:417
  59.8 0.6 %fusion = (f32[8,256]{1,0:T(8,128)}, f32[8,256]{1,0:T(8,128)}) fusion(f32[16,256]{1,0:T(8,128)S(1)} %regression.1), kind=kLoop, calls=%fused_computation | loop fusion | bytes 32768 | tf_op jit(solution)/shard_map/slice | solution.py:460

commit v11 on v10

--- a/solution.py
+++ b/solution.py
@@ -204,7 +204,7 @@
     build(SLAB, 2 * SLAB)
     for step in (3, 2):
         drain(rows.at[pl.ds(0, SLAB)], recv_sem.at[SLABS + step - 1])
-    build(2 * SLAB, LOCAL)
+        build(step * SLAB, (step + 1) * SLAB)
 
     drain(compact_in.at[pl.ds(0, (NX - 1) * ROWS)], recv_sem.at[COMPACT])
     given = jnp.concatenate([compact_in[k * ROWS : (k + 1) * ROWS, :] for k in range(NX)], axis=1)

time: 60.9 us -> 61.1 us (level)
  no operation moved by 1% of the time
where the time goes in v11:
time: 61.1 us; the launch traced here: 60.7 us
  Pallas kernels  59.4 us (97%)
  between operations  0.64 us (1%)
    pallas_call x1, Pallas kernels, body(): pl.pallas_call(kernel, out_shape=jax.ShapeDtypeStruct((16, TARGETS), F32)...  59.4 us

profile of v11, /device:TPU:1, one launch (start us, length us, event | category | flops | bytes accessed | tf_op | source)
XLA Modules:
  0.0 60.7 jit_solution(5731468520161734307)
XLA Ops:
  0.6 59.4 %regression.1 = f32[16,256]{1,0:T(8,128)S(1)} custom-call(bf16[16,256]{1,0:T(8,128)(2,1)} %modes_ref.1, bf16[16,256]{1,0:T(8,128)(2,1)} %targets_ref.1, s32[2,4096]{1,0:T(2,128)} %bitcast.1, s32[8,256]{1,0:T(8,128)} %support_ref.1), custom_call_target="tpu_custom_call" | custom-call | tf_op jit(solution)/shard_map/regression/pallas_call | solution.py:417
  60.1 0.6 fusion
